TPU v7x, 128 devices: a whole 4x4x4 slice. The times are simulated.
128 devices in a mesh: grp: 8 (over z, core), sub: 16 (over y, x).
Axes of the slice: x: 4, y: 4, z: 4, core: 2. Of those that a mesh axis runs over, the one named last changes fastest.
Arguments:
- points: bfloat16 [32768, 1024], P(('grp', 'sub')), may hold values from -20 to 20
- fine_initial: float32 [131072, 1024], P(('grp', 'sub')), may hold values from -6 to 6
- coarse_initial: float32 [16384, 1024], P('sub'), may hold values from -6 to 6
- assign: int32 [2, 32768], P(None, ('grp', 'sub')), may hold values from 0 to 131071, as said below
- parent: int32 [131072], P(('grp', 'sub')), may hold values from 0 to 16383, as said below
Outputs:
- fine_centroids: float32 [131072, 1024], P(('grp', 'sub'))
- coarse_centroids: float32 [16384, 1024], P('sub')
Inputs may be any that keep to these rules, and one draw needn't show every extreme that they name: `assign`: Level-1 centroid k is held by device k // 1024, devices counted in the order grp+sub. In each iteration, among the 256 points of one device at most 4 name centroids held by one device, and some devices receive exactly 4 points from every device. `parent`: Level-2 centroid m lies at sub index m // 1024, in share (m % 1024) // 128 of it. Among the 1024 level-1 centroids of one device at most 128 have parents at one sub index and at most 16 in one share; at every grp index some sub indices receive exactly 128 from every device of that grp index, exactly 16 in each of their shares.
All inputs are finite; a program needn't handle non-finite values.
Results may differ from a plain program's by a relative error of at most 0.0037.
Values may be sent and summed in bfloat16 or wider, within the bound.
No kernel may reach another device: no remote copies, remote signals or barrier semaphores. Data moves between devices by JAX's collectives and lax.ppermute only.
A program may use at most 128 MiB of HBM per device.

v0:
```python
import jax
import jax.numpy as jnp
from jax import lax
from jax.sharding import PartitionSpec as P

ITER2 = 2


def pack_buckets(values, targets, buckets, capacity, owned):
    count_rows = values.shape[0]
    width = values.shape[1]
    owner = targets // owned
    local = targets % owned
    order = jnp.argsort(owner, stable=True)
    sorted_owner = owner[order]
    matches = owner[:, None] == jnp.arange(buckets, dtype=jnp.int32)[None, :]
    counts = jnp.sum(matches.astype(jnp.int32), axis=0)
    starts = jnp.cumsum(counts) - counts
    within = jnp.arange(count_rows, dtype=jnp.int32) - starts[sorted_owner]
    slots = sorted_owner * capacity + within
    rows = jnp.zeros((buckets * capacity, width), values.dtype).at[slots].set(values[order])
    labels = jnp.full((buckets * capacity,), owned, jnp.int32).at[slots].set(local[order])
    return (rows.reshape(buckets, capacity, width), labels.reshape(buckets, capacity))


def weighted_sums(rows, labels, centers):
    owned = centers.shape[0]
    width = rows.shape[1]
    nearest = jnp.take(centers, jnp.minimum(labels, owned - 1), axis=0)
    rows_float = rows.astype(jnp.float32)
    distance = jnp.sum((rows_float - nearest) ** 2, axis=1) / width
    weights = 1.0 / (1.0 + distance)
    scaled = (weights[:, None] * rows_float).astype(jnp.bfloat16)
    member = jnp.arange(owned, dtype=jnp.int32)[:, None] == labels[None, :]
    sums = jnp.dot(member.astype(jnp.bfloat16), scaled, preferred_element_type=jnp.float32)
    mass = jnp.dot(member.astype(jnp.float32), weights, precision=lax.Precision.HIGHEST)
    return (sums, mass)


def shards(points, fine_initial, coarse_initial, assign, parent):
    groups = lax.axis_size("grp")
    sub_count = lax.axis_size("sub")
    devices = groups * sub_count
    width = points.shape[1]
    owned_one = fine_initial.shape[0]
    owned_two = coarse_initial.shape[0]
    capacity = 2 * points.shape[0] // devices
    level_one = fine_initial
    for iteration in range(assign.shape[0]):
        rows, labels = pack_buckets(points, assign[iteration], devices, capacity, owned_one)
        got_rows, got_labels = (
            lax.all_to_all(rows, ("grp", "sub"), split_axis=0, concat_axis=0, tiled=True),
            lax.all_to_all(labels, ("grp", "sub"), split_axis=0, concat_axis=0, tiled=True),
        )
        sums, mass = weighted_sums(got_rows.reshape(-1, width), got_labels.reshape(-1), level_one)
        level_one = (sums + level_one) / (mass + 1.0)[:, None]
    rounded = level_one.astype(jnp.bfloat16)
    capacity_two = 2 * owned_one // sub_count
    rows_two, labels_two = pack_buckets(rounded, parent, sub_count, capacity_two, owned_two)
    got_two, got_labels_two = (
        lax.all_to_all(rows_two, "sub", split_axis=0, concat_axis=0, tiled=True),
        lax.all_to_all(labels_two, "sub", split_axis=0, concat_axis=0, tiled=True),
    )
    flat_rows = got_two.reshape(-1, width)
    flat_labels = got_labels_two.reshape(-1)
    level_two = coarse_initial
    for iteration in range(ITER2):
        sums, mass = weighted_sums(flat_rows, flat_labels, level_two)
        total_sums, total_mass = lax.psum((sums, mass), "grp")
        level_two = (total_sums + level_two) / (total_mass + 1.0)[:, None]
    return (level_one, level_two)


def solution(mesh):
    return jax.shard_map(
        shards,
        mesh=mesh,
        in_specs=(
            P(("grp", "sub"), None),
            P(("grp", "sub"), None),
            P("sub", None),
            P(None, ("grp", "sub")),
            P(("grp", "sub")),
        ),
        out_specs=(P(("grp", "sub"), None), P("sub", None)),
        check_vma=False,
    )
```

profile of v0, /device:TPU:0, one launch (start us, length us, event | category | flops | bytes accessed | tf_op | source)
XLA Modules:
  0.0 454.4 jit_solution(15520597730088309944)
XLA Ops:
  7.2 0.8 fusion.49
  8.1 3.2 sort.48
  11.3 1.9 gather_fusion
  13.2 1.9 gather_fusion.2
  15.3 0.2 reduce-window.27
  15.6 1.9 gather_fusion.1
  17.5 1.4 scatter_custom_fusion
  18.9 0.7 all_to_all.27
  19.6 11.1 %all-to-all-start = ((s32[128,1,4]{2,1,0:T(1,128)}), s32[128,1,4]{2,1,0:T(1,128)S(1)}, u32[]{:S(2)}, u32[]{:S(2)}) async-start(s32[128,1,4]{2,1,0:T(1,128)} %bitcast.6), calls=%async_computation | async-start | bytes 131072 | tf_op jit(solution)/shard_map/all_to_all | solution.py:53
  30.9 3.2 sort.49
  34.1 1.9 gather_fusion.3
  36.2 4.4 sort.50
  40.6 4.5 gather_fusion.6
  45.4 0.7 fusion.50
  46.1 4.4 compare_select_fusion.3
  50.7 0.2 reduce-window.28
  51.0 1.9 gather_fusion.4
  52.9 5.6 %select_select_fusion = s32[1024]{0:T(1024)S(1)} fusion(pred[1024]{0:T(1024)(128)(4,1)S(1)} %get-tuple-element.18, pred[1024]{0:T(1024)(128)(4,1)S(1)} %get-tuple-element.17, pred[1024]{0:T(1024)(128)(4,1)S(1)} %get-tuple-element.16, pred[1024]{0:T(1024)(128)(4,1)S(1)} %get-tuple-element.15, pred[1024]{0:T(1024)(128)(4,1)S(1)} %get-tuple-element.14, ...), kind=kLoop, calls=%fused_computation.120 | loop fusion | flops 9216 | bytes 17444 | tf_op jit(solution)/shard_map/gather | solution.py:19
  58.5 1.9 gather_fusion.5
  60.5 1.4 scatter_custom_fusion.2
  61.9 0.7 all_to_all.30
  62.6 9.8 %all-to-all-start.2 = ((s32[128,1,4]{2,1,0:T(1,128)}), s32[128,1,4]{2,1,0:T(1,128)S(1)}, u32[]{:S(2)}, u32[]{:S(2)}) async-start(s32[128,1,4]{2,1,0:T(1,128)} %bitcast.13), calls=%async_computation.2 | async-start | bytes 131072 | tf_op jit(solution)/shard_map/all_to_all | solution.py:53
  72.4 4.2 scatter_custom_fusion.3
  76.6 3.7 scatter_custom_fusion.1
  80.3 4.5 gather_fusion.7
  84.8 1.2 reshape.349
  86.0 1.2 reshape.346
  87.2 4.9 %scatter_custom_fusion.4 = s32[2048]{0:T(1024)} fusion(s32[1024]{0:T(1024)S(1)} %bitcast.77, s32[1024]{0:T(1024)S(1)} %gather_fusion.7, s32[]{:T(128)} %constant.105.clone.1), kind=kCustom, calls=%fused_computation.122 | custom fusion | bytes 8196 | tf_op jit(solution)/shard_map/scatter | solution.py:22
  92.1 0.5 broadcast.582
  92.6 0.8 reduce.28
  93.5 10.3 %all-to-all-start.3 = ((bf16[128,4,1024]{2,1,0:T(4,128)(2,1)}), bf16[128,4,1024]{2,1,0:T(4,128)(2,1)}, u32[]{:S(2)}, u32[]{:S(2)}) async-start(bf16[128,4,1024]{2,1,0:T(4,128)(2,1)} %reshape.349), calls=%async_computation.3 | async-start | bytes 2097152 | tf_op jit(solution)/shard_map/all_to_all | solution.py:52
  103.9 0.8 reduce.27
  104.8 5.0 %gather_fusion.8 = f32[512,1024]{1,0:T(8,128)S(1)} fusion(f32[1024,1024]{1,0:T(8,128)} %param.10, s32[1024]{0:T(1024)S(1)} %pad_clamp_fusion.1), kind=kCustom, calls=%fused_computation.clone | custom fusion | bytes 4196352 | tf_op jit(solution)/shard_map/jit(_take)/gather | solution.py:29
  109.8 12.6 %all-to-all-done.3 = bf16[128,4,1024]{2,1,0:T(4,128)(2,1)} async-done(((bf16[128,4,1024]{2,1,0:T(4,128)(2,1)}), bf16[128,4,1024]{2,1,0:T(4,128)(2,1)}, u32[]{:S(2)}, u32[]{:S(2)}) %all-to-all-start.3) | async-done | bytes 1048608 | tf_op jit(solution)/shard_map/all_to_all | solution.py:52
  122.5 5.8 %all-to-all-start.1 = ((bf16[128,4,1024]{2,1,0:T(4,128)(2,1)}), bf16[128,4,1024]{2,1,0:T(4,128)(2,1)}, u32[]{:S(2)}, u32[]{:S(2)}) async-start(bf16[128,4,1024]{2,1,0:T(4,128)(2,1)} %reshape.346), calls=%async_computation.1 | async-start | bytes 2097152 | tf_op jit(solution)/shard_map/all_to_all | solution.py:52
  128.2 2.4 reshape.354
  130.7 2.2 fusion.21
  132.8 1.0 fusion.25
  133.9 5.0 %add_divide_fusion.3 = f32[1024,1024]{1,0:T(8,128)} fusion(f32[1024,1024]{1,0:T(8,128)S(1)} %copy-done.2, f32[1024]{0:T(1024)S(1)} %broadcast_add_fusion.3, f32[512,1024]{1,0:T(8,128)} %reshape.354, f32[512]{0:T(512)S(1)} %add_divide_fusion.7, s32[512]{0:T(512)S(1)} %eq.107), kind=kOutput, calls=%fused_computation.45 | convolution fusion | flops 1077411840 | bytes 10493952 | tf_op jit(solution)/shard_map/dot_general | solution.py:35
  138.9 5.0 %gather_fusion.9 = f32[512,1024]{1,0:T(8,128)S(1)} fusion(f32[1024,1024]{1,0:T(8,128)} %add_divide_fusion.3, s32[1024]{0:T(1024)S(1)} %pad_clamp_fusion), kind=kCustom, calls=%fused_computation.2.clone | custom fusion | bytes 4196352 | tf_op jit(solution)/shard_map/jit(_take)/gather | solution.py:29
  143.9 2.9 all-to-all-done.1
  146.9 3.6 all-to-all-start.4
  150.4 2.5 reshape.353
  152.9 2.2 fusion.19
  155.1 1.0 fusion.26
  156.1 5.0 %fusion.51 = (bf16[1024,1024]{1,0:T(8,128)(2,1)S(1)}, f32[1024,1024]{1,0:T(8,128)}) fusion(f32[1024]{0:T(1024)S(1)} %broadcast_add_fusion.2, f32[1024,1024]{1,0:T(8,128)S(1)} %copy-done.3, f32[512,1024]{1,0:T(8,128)} %reshape.353, f32[512]{0:T(512)S(1)} %add_divide_fusion.6, s32[512]{0:T(512)S(1)} %eq.51), kind=kOutput, calls=%fused_computation.156 | convolution fusion | flops 1078460416 | bytes 12591104 | tf_op jit(solution)/shard_map/dot_general | solution.py:35
  161.1 15.3 %scatter_custom_fusion.5 = bf16[2048,1024]{1,0:T(8,128)(2,1)} fusion(s32[1024]{0:T(1024)S(1)} %bitcast.78, bf16[1024,1024]{1,0:T(8,128)(2,1)S(1)} %get-tuple-element.45, s32[1024]{0:T(1024)S(1)} %fusion.40, bf16[]{:T(256)} %constant.116.clone.1), kind=kCustom, calls=%fused_computation.52 | custom fusion | bytes 4194306 | tf_op jit(solution)/shard_map/scatter | solution.py:21
  176.5 7.4 %all-to-all-start.5 = ((bf16[16,128,1024]{2,1,0:T(8,128)(2,1)}), bf16[16,128,1024]{2,1,0:T(8,128)(2,1)}, u32[]{:S(2)}, u32[]{:S(2)}) async-start(bf16[16,128,1024]{2,1,0:T(8,128)(2,1)} %bitcast.60), calls=%async_computation.5 | async-start | bytes 8388608 | tf_op jit(solution)/shard_map/all_to_all | solution.py:61
  183.8 0.3 all-reduce.3.cloned.1.call-start
  184.1 13.9 %gather_fusion.10 = f32[2048,1024]{1,0:T(8,128)} fusion(f32[1024,1024]{1,0:T(8,128)} %param.11, s32[2048]{0:T(1024)S(1)} %fusion.39), kind=kCustom, calls=%fused_computation.1.clone | custom fusion | bytes 16785408 | tf_op jit(solution)/shard_map/jit(_take)/gather | solution.py:29
  198.1 47.8 %all-to-all-done.5 = bf16[16,128,1024]{2,1,0:T(8,128)(2,1)} async-done(((bf16[16,128,1024]{2,1,0:T(8,128)(2,1)}), bf16[16,128,1024]{2,1,0:T(8,128)(2,1)}, u32[]{:S(2)}, u32[]{:S(2)}) %all-to-all-start.5) | async-done | bytes 4194336 | tf_op jit(solution)/shard_map/all_to_all | solution.py:61
  245.9 5.6 %fusion.1 = f32[2048]{0:T(1024)S(1)} fusion(f32[2048,1024]{1,0:T(8,128)} %gather_fusion.10, bf16[16,128,1024]{2,1,0:T(8,128)(2,1)} %all-to-all-done.5, pred[2048]{0:T(1024)(128)(4,1)S(1)} %compare_and_fusion), kind=kLoop, calls=%fused_computation.26 | loop fusion | flops 10483712 | bytes 12593152 | tf_op jit(solution)/shard_map/reduce_sum | solution.py:31
  251.5 8.4 %fusion.9 = f32[1024,1024]{1,0:T(8,128)} fusion(bf16[2048,1024]{1,0:T(8,128)(2,1)} %bitcast.43, f32[2048]{0:T(1024)S(1)} %add_divide_fusion.5, s32[2048]{0:T(1024)S(1)} %bitcast.63), kind=kOutput, calls=%fused_computation.35 | convolution fusion | flops 4303355904 | bytes 8404992 | tf_op jit(solution)/shard_map/dot_general | solution.py:35
  260.0 3.8 fusion.8
  263.8 14.5 %psum.29 = f32[1024]{0:T(1024)S(1)} all-reduce(f32[1024]{0:T(1024)S(1)} %bitcast.82), channel_id=1, replica_groups=mesh['grp'=8,'sub'=16] {'grp'}, use_global_device_ids=true, to_apply=%region_19.22 | all-reduce | flops 1024 | bytes 8192 | tf_op jit(solution)/shard_map/psum | solution.py:69
  278.3 54.6 %all-reduce.3.cloned.1.call-done = f32[1024,1024]{1,0:T(8,128)} async-done(((f32[1024,1024]{1,0:T(8,128)}), f32[1024,1024]{1,0:T(8,128)}) %all-reduce.3.cloned.1.call-update) | async-done | bytes 4194320 | tf_op jit(solution)/shard_map/psum | solution.py:69
  332.9 6.7 %add_divide_fusion.1 = f32[1024,1024]{1,0:T(8,128)} fusion(f32[1024,1024]{1,0:T(8,128)} %all-reduce.3.cloned.1.call-done, f32[1024,1024]{1,0:T(8,128)} %param.11, f32[1024]{0:T(1024)S(1)} %broadcast_add_fusion.1), kind=kLoop, calls=%fused_computation.38 | loop fusion | flops 2097152 | bytes 12587008 | tf_op jit(solution)/shard_map/div | solution.py:70
  339.6 13.9 %gather_fusion.11 = f32[2048,1024]{1,0:T(8,128)} fusion(f32[1024,1024]{1,0:T(8,128)} %add_divide_fusion.1, s32[2048]{0:T(1024)S(1)} %fusion.39), kind=kCustom, calls=%fused_computation.3.clone | custom fusion | bytes 16785408 | tf_op jit(solution)/shard_map/jit(_take)/gather | solution.py:29
  353.5 5.6 %fusion.4 = f32[2048]{0:T(1024)S(1)} fusion(f32[2048,1024]{1,0:T(8,128)} %gather_fusion.11, bf16[16,128,1024]{2,1,0:T(8,128)(2,1)} %all-to-all-done.5, pred[2048]{0:T(1024)(128)(4,1)S(1)} %compare_and_fusion), kind=kLoop, calls=%fused_computation.29 | loop fusion | flops 10483712 | bytes 12593152 | tf_op jit(solution)/shard_map/reduce_sum | solution.py:31
  359.1 8.4 %fusion.7 = f32[1024,1024]{1,0:T(8,128)} fusion(bf16[2048,1024]{1,0:T(8,128)(2,1)} %bitcast.43, f32[2048]{0:T(1024)S(1)} %add_divide_fusion.4, s32[2048]{0:T(1024)S(1)} %bitcast.65), kind=kOutput, calls=%fused_computation.33 | convolution fusion | flops 4303355904 | bytes 8404992 | tf_op jit(solution)/shard_map/dot_general | solution.py:35
  367.6 3.8 fusion.6
  371.3 14.1 %psum.31 = f32[1024]{0:T(1024)S(1)} all-reduce(f32[1024]{0:T(1024)S(1)} %bitcast.81), channel_id=1, replica_groups=mesh['grp'=8,'sub'=16] {'grp'}, use_global_device_ids=true, to_apply=%region_22.25 | all-reduce | flops 1024 | bytes 8192 | tf_op jit(solution)/shard_map/psum | solution.py:69
  385.5 55.0 %all-reduce.5.cloned.1.call-done = f32[1024,1024]{1,0:T(8,128)} async-done(((f32[1024,1024]{1,0:T(8,128)}), f32[1024,1024]{1,0:T(8,128)}) %all-reduce.5.cloned.1.call-update) | async-done | bytes 4194320 | tf_op jit(solution)/shard_map/psum | solution.py:69
  440.4 6.7 %add_divide_fusion = f32[1024,1024]{1,0:T(8,128)} fusion(f32[1024,1024]{1,0:T(8,128)} %all-reduce.5.cloned.1.call-done, f32[1024,1024]{1,0:T(8,128)} %add_divide_fusion.1, f32[1024]{0:T(1024)S(1)} %broadcast_add_fusion), kind=kLoop, calls=%fused_computation.36 | loop fusion | flops 2097152 | bytes 12587008 | tf_op jit(solution)/shard_map/div | solution.py:70
  (66 shorter events, 1.7 us)
Async XLA Ops:
  7.2 65.2 %copy-start = (bf16[256,1024]{1,0:T(8,128)(2,1)S(1)}, bf16[256,1024]{1,0:T(8,128)(2,1)}, u32[]{:S(2)}) copy-start(bf16[256,1024]{1,0:T(8,128)(2,1)} %param.9) | copy-start | bytes 1572868
  7.2 28.9 %copy-start.4 = (s32[1024]{0:T(1024)S(1)}, s32[1024]{0:T(1024)}, u32[]{:S(2)}) copy-start(s32[1024]{0:T(1024)} %param.13) | copy-start | bytes 12292
  19.6 43.0 %all-to-all-start = ((s32[128,1,4]{2,1,0:T(1,128)}), s32[128,1,4]{2,1,0:T(1,128)S(1)}, u32[]{:S(2)}, u32[]{:S(2)}) async-start(s32[128,1,4]{2,1,0:T(1,128)} %bitcast.6), calls=%async_computation | async-start | bytes 131072 | tf_op jit(solution)/shard_map/all_to_all | solution.py:53
  62.6 30.9 %all-to-all-start.2 = ((s32[128,1,4]{2,1,0:T(1,128)}), s32[128,1,4]{2,1,0:T(1,128)S(1)}, u32[]{:S(2)}, u32[]{:S(2)}) async-start(s32[128,1,4]{2,1,0:T(1,128)} %bitcast.13), calls=%async_computation.2 | async-start | bytes 131072 | tf_op jit(solution)/shard_map/all_to_all | solution.py:53
  93.5 28.9 %all-to-all-start.3 = ((bf16[128,4,1024]{2,1,0:T(4,128)(2,1)}), bf16[128,4,1024]{2,1,0:T(4,128)(2,1)}, u32[]{:S(2)}, u32[]{:S(2)}) async-start(bf16[128,4,1024]{2,1,0:T(4,128)(2,1)} %reshape.349), calls=%async_computation.3 | async-start | bytes 2097152 | tf_op jit(solution)/shard_map/all_to_all | solution.py:52
  122.5 24.4 %all-to-all-start.1 = ((bf16[128,4,1024]{2,1,0:T(4,128)(2,1)}), bf16[128,4,1024]{2,1,0:T(4,128)(2,1)}, u32[]{:S(2)}, u32[]{:S(2)}) async-start(bf16[128,4,1024]{2,1,0:T(4,128)(2,1)} %reshape.346), calls=%async_computation.1 | async-start | bytes 2097152 | tf_op jit(solution)/shard_map/all_to_all | solution.py:52
  130.7 3.2 copy-start.2
  146.9 29.6 %all-to-all-start.4 = ((s32[16,1,128]{2,1,0:T(1,128)}), s32[16,1,128]{2,1,0:T(1,128)S(1)}, u32[]{:S(2)}, u32[]{:S(2)}) async-start(s32[16,1,128]{2,1,0:T(1,128)} %bitcast.39), calls=%async_computation.4 | async-start | bytes 16384 | tf_op jit(solution)/shard_map/all_to_all | solution.py:62
  152.9 3.2 copy-start.3
  176.5 69.4 %all-to-all-start.5 = ((bf16[16,128,1024]{2,1,0:T(8,128)(2,1)}), bf16[16,128,1024]{2,1,0:T(8,128)(2,1)}, u32[]{:S(2)}, u32[]{:S(2)}) async-start(bf16[16,128,1024]{2,1,0:T(8,128)(2,1)} %bitcast.60), calls=%async_computation.5 | async-start | bytes 8388608 | tf_op jit(solution)/shard_map/all_to_all | solution.py:61
  183.8 149.0 %all-reduce.3.cloned.1.call-start = ((), (), s32[]{:S(2)}) async-start(), calls=%async_computation.6 | async-start | bytes 8388608 | tf_op jit(solution)/shard_map/psum | solution.py:69
  260.0 180.5 %all-reduce.5.cloned.1.call-start = ((), (), s32[]{:S(2)}) async-start(), calls=%async_computation.7 | async-start | bytes 8388608 | tf_op jit(solution)/shard_map/psum | solution.py:69
  385.4 61.7 %copy-start.1 = (bf16[256,1024]{1,0:T(8,128)(2,1)S(1)}, bf16[256,1024]{1,0:T(8,128)(2,1)}, u32[]{:S(2)}) copy-start(bf16[256,1024]{1,0:T(8,128)(2,1)} %param.9) | copy-start | bytes 1572868
Sparse Core Ops, SparseCore 0:
  260.1 72.7 all-reduce.2
  367.7 72.7 all-reduce.4
where the time goes:
time: 463 us; the launch traced here: 454 us
  waiting for transfers between devices  173 us (37%)
  local copies, waits for them, and re-layouts  101 us (22%)
  other arithmetic  52.5 us (11%)
  starting transfers between devices  48.2 us (10%)
  matrix products  36.5 us (8%)
  blocking collectives  28.6 us (6%)
  between operations  14.9 us (3%)
    psum x2, waiting for transfers between devices, shards(): total_sums, total_mass = lax.psum((sums, mass), 'grp')  110 us
    all_to_all x1, waiting for transfers between devices, shards(): lax.all_to_all(rows_two, 'sub', split_axis=0, concat_axis=0, tiled=True)  47.8 us
    gather x4, local copies, waits for them, and re-layouts, weighted_sums(): nearest = jnp.take(centers, jnp.minimum(labels, owned - 1), axis=0)  37.9 us
    psum x2, blocking collectives, shards(): total_sums, total_mass = lax.psum((sums, mass), 'grp')  28.6 us
    dot_general x4, matrix products, weighted_sums(): jnp.dot(member.astype(jnp.bfloat16), scaled, preferred_element_type=jnp.f...  26.9 us
    scatter x3, local copies, waits for them, and re-layouts, pack_buckets(): jnp.zeros((buckets * capacity, width), values.dtype).at[slots]  23.2 us
    all_to_all x2, starting transfers between devices, shards(): lax.all_to_all(labels, ('grp', 'sub'), split_axis=0, concat_axis=0, tiled...  20.9 us
    all_to_all x2, starting transfers between devices, shards(): lax.all_to_all(rows, ('grp', 'sub'), split_axis=0, concat_axis=0, tiled=T...  16.1 us
  transfers between devices with their start and end apart: 8, of which 5 were waited for; matrix products, arithmetic and copies ran while one was open for 27% of the time, Pallas kernels for 0%

commit v1 on v0

v1 whole, which is shorter than its diff:
```python
import jax
import jax.numpy as jnp
from jax import lax
from jax.experimental import pallas as pl
from jax.experimental.pallas import tpu as pltpu
from jax.sharding import PartitionSpec as P

ITER2 = 2
CAP = 4
CAP_SHARE = 16
EXTRA = 128
DIGIT = 32
F32 = jnp.float32
BF16 = jnp.bfloat16
TURNS = (2, 1, 3)
PACK_MIB = 16
ONE_MIB = 36
TWO_MIB = 24
PLACE_MIB = 16


def nt(a, b):
    return lax.dot_general(a, b, (((1,), (1,)), ((), ())), preferred_element_type=F32)


def tn(a, b):
    return lax.dot_general(a, b, (((0,), (0,)), ((), ())), preferred_element_type=F32)


def nn(a, b):
    return lax.dot_general(a, b, (((1,), (0,)), ((), ())), preferred_element_type=F32)


def iota(shape, dim):
    return lax.broadcasted_iota(jnp.int32, shape, dim)


def onehot(mask):
    return jnp.where(mask, 1.0, 0.0).astype(BF16)


def split2(x):
    hi = x.astype(BF16)
    lo = (x - hi.astype(F32)).astype(BF16)
    return hi, lo


def rank_in_bucket(member):
    n = member.shape[1]
    step = 128
    ones = jnp.where(member, 1.0, 0.0)
    earlier = onehot(iota((step, step), 0) < iota((step, step), 1))
    seen = jnp.zeros((member.shape[0], 1), F32)
    ranks = []
    for c in range(0, n, step):
        block = ones[:, c : c + step]
        before = nn(block.astype(BF16), earlier) + seen
        ranks.append(jnp.sum(block * before, axis=0, keepdims=True))
        seen = seen + jnp.sum(block, axis=1, keepdims=True)
    return jnp.concatenate(ranks, axis=1).astype(jnp.int32)


def pack_one_kernel(
    devices, owned, share, subs, assign_hbm, parent_hbm, points_hbm, out_ref, slot_ref, assign_ref, parent_ref, points_ref, sems
):
    copies = [
        pltpu.make_async_copy(parent_hbm, parent_ref, sems.at[0]),
        pltpu.make_async_copy(assign_hbm, assign_ref, sems.at[1]),
        pltpu.make_async_copy(points_hbm, points_ref, sems.at[2]),
    ]
    for copy in copies:
        copy.start()
    copies[0].wait()
    iters, n = assign_ref.shape
    group = CAP * iters
    slots = devices * group
    width = points_ref.shape[1]

    parent = parent_ref[...]
    k = parent.shape[1]
    per_sub = share * (devices // subs)
    dest = (parent % per_sub) // share * subs + parent // per_sub
    member = iota((devices, k), 0) == dest
    rank = rank_in_bucket(member)
    slot_ref[...] = dest * CAP_SHARE + rank
    lane = iota((EXTRA, k), 0)
    labels = jnp.where(lane == CAP_SHARE + rank, parent % share + 1, 0)
    labels = nt(onehot(member), labels.astype(F32).astype(BF16)).astype(BF16)
    spread = onehot(iota((slots, devices), 0) == iota((slots, devices), 1) * group)
    extra = nn(spread, labels)

    copies[1].wait()
    hot = None
    slot_iota = iota((slots, n), 0)
    for t in range(iters):
        target = assign_ref[t : t + 1, :]
        dest = target // owned
        local = target % owned
        rank = rank_in_bucket(iota((devices, n), 0) == dest)
        mask = slot_iota == dest * group + t * CAP + rank
        hot = mask if hot is None else jnp.logical_or(hot, mask)
        lane = iota((EXTRA, n), 0)
        digits = jnp.where(lane == 0, local // DIGIT + 1, jnp.where(lane == 1, local % DIGIT, 0))
        extra = extra + nt(onehot(mask), digits.astype(F32).astype(BF16))
    out_ref[:, width:] = extra.astype(BF16)
    copies[2].wait()
    out_ref[:, :width] = nn(onehot(hot), points_ref[...]).astype(BF16)


def lloyd_one_kernel(
    iters, index_ref, got_ref, centers_ref, slot_ref, coarse_hbm, out_hbm, send_ref, two_ref, share_ref, out_ref, scaled_ref, member_ref, sems
):
    share = share_ref.shape[0]
    start = pl.multiple_of(index_ref[0] * share, share)
    share_copy = pltpu.make_async_copy(coarse_hbm.at[pl.ds(start, share)], share_ref, sems.at[0])
    share_copy.start()
    owned, width = centers_ref.shape
    group = CAP * iters
    total = got_ref.shape[0]
    half = total // 2
    step = 128
    member_two(group, got_ref, two_ref)
    low = iota((step, EXTRA), 0) % 8 < CAP
    wide_low = iota((step, width), 0) % 8 < CAP
    for t in range(iters):
        old_ref = centers_ref if t == 0 else out_ref
        rounded = old_ref[...].astype(BF16)
        mass = jnp.zeros((owned, EXTRA), F32)
        for c in range(0, half, step):
            def rows(lo, hi, keep):
                got = got_ref[2 * c : 2 * (c + step), lo:hi].astype(F32).reshape(step // 8, 16, hi - lo)
                even = got[:, 0:8, :].reshape(step, hi - lo)
                odd = got[:, 8:16, :].reshape(step, hi - lo)
                if t == 0:
                    return jnp.where(keep, even, pltpu.roll(odd, CAP, 0))
                return jnp.where(keep, pltpu.roll(even, step - CAP, 0), odd)

            extra = rows(width, width + EXTRA, low)
            values = rows(0, width, wide_low)
            label = ((extra[:, 0:1] - 1.0) * DIGIT + extra[:, 1:2]).astype(jnp.int32)
            member = onehot(iota((step, owned), 1) == label)
            member_ref[c : c + step, :] = member
            nearest = nn(member, rounded)
            distance = jnp.sum((values - nearest) ** 2, axis=1, keepdims=True) / width
            weights = 1.0 / (1.0 + distance)
            scaled_ref[c : c + step, :width] = (weights * values).astype(BF16)
            scaled_ref[c : c + step, width:] = weight_columns(weights)
        member = member_ref[...]
        mass = tn(member, scaled_ref[:, width:])
        scale = 1.0 / (jnp.sum(mass, axis=1, keepdims=True) + 1.0)
        out_ref[...] = (tn(member, scaled_ref[:, :width]) + old_ref[...]) * scale
    out_copy = pltpu.make_async_copy(out_ref, out_hbm, sems.at[1])
    out_copy.start()
    rounded = out_ref[...].astype(BF16)
    slots = send_ref.shape[0]
    step = 256
    for s in range(0, slots, step):
        pick = onehot(iota((step, owned), 0) + s == slot_ref[...])
        send_ref[s : s + step, :] = nn(pick, rounded).astype(BF16)
    share_copy.wait()
    out_copy.wait()


def weight_columns(weights):
    n = weights.shape[0]
    hi = weights.astype(BF16).astype(F32)
    mid = (weights - hi).astype(BF16).astype(F32)
    low = weights - hi - mid
    lane = iota((n, 128), 1)
    cols = jnp.where(lane == 0, hi, jnp.where(lane == 1, mid, jnp.where(lane == 2, low, 0.0)))
    return cols.astype(BF16)


def member_two(group, got_ref, member_ref):
    total, share = member_ref.shape
    slots = got_ref.shape[0]
    devices = slots // group
    first = onehot(iota((devices, slots), 1) == iota((devices, slots), 0) * group)
    labels = nn(first, got_ref[:, got_ref.shape[1] - EXTRA :]).astype(BF16)
    expand = onehot(iota((total, devices), 0) // CAP_SHARE == iota((total, devices), 1))
    labels = nn(expand, labels)
    mine = iota((total, EXTRA), 1) == CAP_SHARE + iota((total, EXTRA), 0) % CAP_SHARE
    label = jnp.sum(jnp.where(mine, labels, 0.0), axis=1, keepdims=True).astype(jnp.int32) - 1
    member_ref[...] = onehot(iota((total, share), 1) == label)


def lloyd_two_kernel(got_ref, member_ref, centers_ref, out_ref, norm_ref, weighted_ref):
    share, width = centers_ref.shape
    total = got_ref.shape[0]
    step = 256
    centers = centers_ref[...]
    diagonal = iota((share, share), 0) == iota((share, share), 1)
    for t in range(ITER2):
        hi, lo = split2(centers)
        both = jnp.concatenate([hi, lo], axis=0)
        squares = jnp.sum(centers * centers, axis=1, keepdims=True)
        squares = jnp.sum(jnp.where(diagonal, squares, 0.0), axis=0, keepdims=True)
        for c in range(0, total, step):
            rows = got_ref[c : c + step, :]
            member = member_ref[c : c + step, :].astype(F32)
            if t == 0:
                values = rows.astype(F32)
                norm_ref[c : c + step, :] = jnp.sum(values * values, axis=1, keepdims=True)
            cross = nt(rows, both)
            cross = cross[:, :share] + cross[:, share:]
            rest = jnp.sum(member * (squares - 2.0 * cross), axis=1, keepdims=True)
            distance = jnp.maximum(norm_ref[c : c + step, :] + rest, 0.0) / width
            weights = member / (1.0 + distance)
            hi, lo = split2(weights)
            weighted_ref[c : c + step, :share] = hi
            weighted_ref[c : c + step, share:] = lo
        weighted = weighted_ref[...]
        sums = tn(weighted, got_ref[...])
        mass = tn(weighted, jnp.ones((total, 128), BF16))
        scale = 1.0 / (mass[:share, :1] + mass[share:, :1] + 1.0)
        centers = (sums[:share] + sums[share:] + centers) * scale
    out_ref[...] = centers.astype(BF16)


def place_kernel(places, groups, index_ref, *refs):
    blocks = refs[: len(places)]
    out_hbm, wide_ref, sems = refs[-3:]
    rows = blocks[0].shape[0]
    copies = []
    for i, (ref, (turn, flip)) in enumerate(zip(blocks, places)):
        wide_ref[i] = ref[...].astype(F32)
        held = lax.rem(index_ref[0] + groups - 2 * turn, groups)
        held = held + flip * (1 - 2 * lax.rem(held, 2))
        at = pl.multiple_of(held * rows, rows)
        copies.append(pltpu.make_async_copy(wide_ref.at[i], out_hbm.at[pl.ds(at, rows)], sems.at[i]))
        copies[-1].start()
    for copy in copies:
        copy.wait()


def whole():
    return pl.BlockSpec(memory_space=pltpu.VMEM)


def in_hbm():
    return pl.BlockSpec(memory_space=pltpu.HBM)


def keep_in_hbm(x):
    return pltpu.with_memory_space_constraint(x, pltpu.HBM)


def params(mib):
    return pltpu.CompilerParams(vmem_limit_bytes=mib * 1024 * 1024)


def pack_points(devices, subs, owned, share, assign, parent, points):
    iters = assign.shape[0]
    return pl.pallas_call(
        lambda *refs: pack_one_kernel(devices, owned, share, subs, *refs),
        out_shape=(
            jax.ShapeDtypeStruct((devices * CAP * iters, points.shape[1] + EXTRA), BF16),
            jax.ShapeDtypeStruct(parent.shape, jnp.int32),
        ),
        in_specs=[in_hbm()] * 3,
        out_specs=(whole(), whole()),
        scratch_shapes=[
            pltpu.VMEM(assign.shape, assign.dtype),
            pltpu.VMEM(parent.shape, parent.dtype),
            pltpu.VMEM(points.shape, points.dtype),
            pltpu.SemaphoreType.DMA((3,)),
        ],
        compiler_params=params(PACK_MIB),
        name="pack_points",
    )(keep_in_hbm(assign), keep_in_hbm(parent), keep_in_hbm(points))


def level_one(iters, devices, share, index, got, centers, slot_two, coarse):
    owned, width = centers.shape
    half = got.shape[0] // 2
    slots_two = devices * CAP_SHARE
    return pl.pallas_call(
        lambda *refs: lloyd_one_kernel(iters, *refs),
        out_shape=(
            pltpu.HBM((owned, width), F32),
            jax.ShapeDtypeStruct((slots_two, width), BF16),
            jax.ShapeDtypeStruct((slots_two, share), BF16),
            jax.ShapeDtypeStruct((share, width), F32),
        ),
        in_specs=[pl.BlockSpec(memory_space=pltpu.SMEM)] + [whole()] * 3 + [in_hbm()],
        out_specs=(in_hbm(), whole(), whole(), whole()),
        scratch_shapes=[
            pltpu.VMEM((owned, width), F32),
            pltpu.VMEM((half, width + EXTRA), BF16),
            pltpu.VMEM((half, owned), BF16),
            pltpu.SemaphoreType.DMA((2,)),
        ],
        compiler_params=params(ONE_MIB),
        name="level_one",
    )(index, got, centers, slot_two, keep_in_hbm(coarse))


def level_two(got, member, centers):
    slots, width = got.shape
    share = centers.shape[0]
    return pl.pallas_call(
        lloyd_two_kernel,
        out_shape=jax.ShapeDtypeStruct((share, width), BF16),
        in_specs=[whole()] * 3,
        out_specs=whole(),
        scratch_shapes=[
            pltpu.VMEM((slots, 1), F32),
            pltpu.VMEM((slots, 2 * share), BF16),
        ],
        compiler_params=params(TWO_MIB),
        name="level_two",
    )(got, member, centers)


def place(groups, index, blocks, out=None):
    places, arrays = list(blocks), list(blocks.values())
    share, width = arrays[0].shape
    extra = [] if out is None else [out]
    return pl.pallas_call(
        lambda *refs: place_kernel(places, groups, *refs),
        out_shape=pltpu.HBM((groups * share, width), F32),
        in_specs=[pl.BlockSpec(memory_space=pltpu.SMEM)] + [whole()] * len(arrays) + [in_hbm()] * len(extra),
        out_specs=in_hbm(),
        scratch_shapes=[pltpu.VMEM((len(arrays), share, width), F32), pltpu.SemaphoreType.DMA((len(arrays),))],
        input_output_aliases={1 + len(arrays): 0} if extra else {},
        compiler_params=params(PLACE_MIB),
        name="place_shares",
    )(index, *arrays, *extra)


def gather_shares(own, groups, index):
    blocks = {(0, 0): own}
    for k in TURNS:
        blocks[(k, 0)] = lax.ppermute(own, "grp", [(g, (g + 2 * k) % groups) for g in range(groups)])
    for k in (0, *TURNS):
        blocks[(k, 1)] = lax.ppermute(blocks[(k, 0)], "grp", [(g, g ^ 1) for g in range(groups)])
    last = TURNS[-1]
    out = place(groups, index, {p: b for p, b in blocks.items() if p[0] != last})
    return place(groups, index, {p: b for p, b in blocks.items() if p[0] == last}, out)


def shards(points, fine_initial, coarse_initial, assign, parent):
    groups = lax.axis_size("grp")
    subs = lax.axis_size("sub")
    devices = groups * subs
    iters = assign.shape[0]
    width = points.shape[1]
    owned = fine_initial.shape[0]
    share = coarse_initial.shape[0] // groups
    slots_two = devices * CAP_SHARE

    me = lax.axis_index("grp").astype(jnp.int32).reshape(1)
    send, slot_two = pack_points(devices, subs, owned, share, assign, parent.reshape(1, owned), points)
    send, me = lax.optimization_barrier((send, me))
    got = lax.all_to_all(
        send.reshape(devices, CAP * iters, width + EXTRA), ("grp", "sub"), split_axis=0, concat_axis=0, tiled=True
    ).reshape(devices * CAP * iters, width + EXTRA)
    fine, send_two, member, centers = level_one(
        iters, devices, share, me, got, fine_initial, slot_two, coarse_initial
    )
    got_two = lax.all_to_all(
        send_two.reshape(devices, CAP_SHARE, width), ("grp", "sub"), split_axis=0, concat_axis=0, tiled=True
    ).reshape(slots_two, width)
    own = level_two(got_two, member, centers)
    return fine, gather_shares(own, groups, me)


def solution(mesh):
    return jax.shard_map(
        shards,
        mesh=mesh,
        in_specs=(
            P(("grp", "sub"), None),
            P(("grp", "sub"), None),
            P("sub", None),
            P(None, ("grp", "sub")),
            P(("grp", "sub")),
        ),
        out_specs=(P(("grp", "sub"), None), P("sub", None)),
        check_vma=False,
    )
```

time: 463 us -> 143 us (0.31); the launches traced: 454 us -> 142 us
  waiting for transfers between devices: 173 us -> 11.8 us
  local copies, waits for them, and re-layouts: 101 us -> 0.01 us
  blocking collectives: 28.6 us -> 99.1 us
  other arithmetic: 52.5 us -> 0 us
  starting transfers between devices: 48.2 us -> 5.48 us
  matrix products: 36.5 us -> 0 us
  Pallas kernels: 0 us -> 24.8 us
  between operations: 14.9 us -> 0.87 us
    psum x2 -> x0, waiting for transfers between devices: 110 us -> none  [shards(): total_sums, total_mass = lax.psum((sums, mass), 'grp')]
    all_to_all x0 -> x2, blocking collectives: none -> 99.1 us  [the longest x1 55.9 us: shards(): lax.all_to_all(send_two.reshape(devices, CAP_SHARE, width), ('grp', 'sub'...]
    all_to_all x6 -> x0, waiting for transfers between devices: 63.4 us -> none  [the longest x1 47.8 us: shards(): lax.all_to_all(rows_two, 'sub', split_axis=0, concat_axis=0, tiled=True)]
    gather x13 -> x0, local copies, waits for them, and re-layouts: 59.2 us -> none  [the longest x4 37.9 us: weighted_sums(): nearest = jnp.take(centers, jnp.minimum(labels, owned - 1), axis=0)]
    all_to_all x6 -> x0, starting transfers between devices: 47.9 us -> none  [the longest x2 20.9 us: shards(): lax.all_to_all(labels, ('grp', 'sub'), split_axis=0, concat_axis=0, tiled...]
    dot_general x8 -> x0, matrix products: 36.5 us -> none  [the longest x4 26.9 us: weighted_sums(): jnp.dot(member.astype(jnp.bfloat16), scaled, preferred_element_type=jnp.f...]
    scatter x6 -> x0, local copies, waits for them, and re-layouts: 30.9 us -> none  [the longest x3 23.2 us: pack_buckets(): jnp.zeros((buckets * capacity, width), values.dtype).at[slots]]
    psum x2 -> x0, blocking collectives: 28.6 us -> none  [shards(): total_sums, total_mass = lax.psum((sums, mass), 'grp')]
  transfers between devices with their start and end apart: 8 -> 7, of which waited for: 5 -> 4; matrix products, arithmetic and copies ran while one was open for 27% -> 0% of each run, Pallas kernels for 0% -> 1%
where the time goes in v1:
time: 143 us; the launch traced here: 142 us
  blocking collectives  99.1 us (69%)
  Pallas kernels  24.8 us (17%)
  waiting for transfers between devices  11.8 us (8%)
  starting transfers between devices  5.48 us (4%)
    all_to_all x1, blocking collectives, shards(): lax.all_to_all(send_two.reshape(devices, CAP_SHARE, width), ('grp', 'sub'...  55.9 us
    all_to_all x1, blocking collectives, shards(): lax.all_to_all(send.reshape(devices, CAP * iters, width + EXTRA), ('grp',...  43.3 us
    pallas_call x1, Pallas kernels, level_one(): pl.pallas_call(lambda *refs: lloyd_one_kernel(iters, *refs), out_shape=(p...  12.8 us
    ppermute x3, waiting for transfers between devices, gather_shares(): lax.ppermute(own, 'grp', [(g, (g + 2 * k) % groups) for g in range(groups)])  10.5 us
    pallas_call x1, Pallas kernels, level_two(): pl.pallas_call(lloyd_two_kernel, out_shape=jax.ShapeDtypeStruct((share, w...  6.34 us
    ppermute x3, starting transfers between devices, gather_shares(): lax.ppermute(own, 'grp', [(g, (g + 2 * k) % groups) for g in range(groups)])  4.96 us
    pallas_call x1, Pallas kernels, pack_points(): pl.pallas_call(lambda *refs: pack_one_kernel(devices, owned, share, subs,...  2.91 us
  transfers between devices with their start and end apart: 7, of which 4 were waited for; matrix products, arithmetic and copies ran while one was open for 0% of the time, Pallas kernels for 1%

profile of v1, /device:TPU:0, one launch (start us, length us, event | category | flops | bytes accessed | tf_op | source)
XLA Modules:
  0.0 142.1 jit_solution(12553759416933740861)
XLA Ops:
  0.6 0.0 copy-start
  0.6 2.9 %pack_points.1 = (bf16[1024,1152]{1,0:T(8,128)(2,1)S(1)}, s32[1,1024]{1,0:T(1,128)S(1)}) custom-call(s32[2,256]{1,0:T(2,128)} %refs_0_.1, s32[1,1024]{1,0:T(1,128)} %bitcast.10, bf16[256,1024]{1,0:T(8,128)(2,1)} %refs_2_.2), custom_call_target="tpu_custom_call" | custom-call | tf_op jit(solution)/shard_map/pack_points/pallas_call | solution.py:254
  3.6 43.3 %all_to_all.10 = bf16[128,8,1152]{2,1,0:T(8,128)(2,1)S(1)} all-to-all(bf16[128,8,1152]{2,1,0:T(8,128)(2,1)S(1)} %bitcast.9), channel_id=1, replica_groups=mesh['grp'=8,'sub'=16] {'grp','sub'}, dimensions={0} | all-to-all | bytes 4718592 | tf_op jit(solution)/shard_map/all_to_all | solution.py:355
  46.9 0.0 copy-done
  46.9 12.8 %level_one.1 = (f32[1024,1024]{1,0:T(8,128)}, bf16[2048,1024]{1,0:T(8,128)(2,1)S(1)}, bf16[2048,128]{1,0:T(8,128)(2,1)S(1)}, f32[128,1024]{1,0:T(8,128)S(1)}) custom-call(s32[1]{0:T(128)} %bitcast.1.refs_0_, bf16[1024,1152]{1,0:T(8,128)(2,1)S(1)} %bitcast.7, f32[1024,1024]{1,0:T(8,128)S(1)} %copy-done, s32[1,1024]{1,0:T(1,128)S(1)} %get-tuple-element.13.refs_3_, ...), custom_call_target="tpu_custom_call" | custom-call | tf_op jit(solution)/shard_map/level_one/pallas_call | solution.py:277
  59.7 55.9 %all_to_all.11 = bf16[128,16,1024]{2,1,0:T(8,128)(2,1)S(1)} all-to-all(bf16[128,16,1024]{2,1,0:T(8,128)(2,1)S(1)} %bitcast.8), channel_id=1, replica_groups=mesh['grp'=8,'sub'=16] {'grp','sub'}, dimensions={0} | all-to-all | bytes 8388608 | tf_op jit(solution)/shard_map/all_to_all | solution.py:361
  115.5 6.3 %level_two.1.refs_1_ = bf16[128,1024]{1,0:T(8,128)(2,1)S(1)} custom-call(bf16[2048,1024]{1,0:T(8,128)(2,1)S(1)} %bitcast.6, bf16[2048,128]{1,0:T(8,128)(2,1)S(1)} %get-tuple-element.16.member_ref, f32[128,1024]{1,0:T(8,128)S(1)} %get-tuple-element.17.centers_ref), custom_call_target="tpu_custom_call" | custom-call | tf_op jit(solution)/shard_map/level_two/pallas_call | solution.py:301
  121.9 0.9 collective-permute-start.3
  122.8 2.8 %collective-permute-start.2 = (bf16[128,1024]{1,0:T(8,128)(2,1)S(1)}, bf16[128,1024]{1,0:T(8,128)(2,1)S(1)}, u32[]{:S(2)}, u32[]{:S(2)}) collective-permute-start(bf16[128,1024]{1,0:T(8,128)(2,1)S(1)} %level_two.1.refs_1_), channel_id=1, source_target_pairs={{0,64},{16,80},{32,96},{48,112},{64,0},{80,16},{96,32},{112,48},{1... | collective-permute-start | bytes 786440 | tf_op jit(solution)/shard_map/ppermute | solution.py:334
  125.6 1.2 collective-permute-start
  126.8 0.0 collective-permute-start.4
  126.8 10.4 %collective-permute-done.3.refs_3_ = bf16[128,1024]{1,0:T(8,128)(2,1)S(1)} collective-permute-done((bf16[128,1024]{1,0:T(8,128)(2,1)S(1)}, bf16[128,1024]{1,0:T(8,128)(2,1)S(1)}, u32[]{:S(2)}, u32[]{:S(2)}) %collective-permute-start.3) | collective-permute-done | bytes 262176 | tf_op jit(solution)/shard_map/ppermute | solution.py:334
  137.2 0.0 collective-permute-start.6
  137.2 0.0 collective-permute-done.2.refs_2_
  137.2 0.5 collective-permute-start.5
  137.8 0.1 collective-permute-done.refs_1_
  137.9 0.0 collective-permute-start.1
  137.9 0.0 collective-permute-done.4.refs_4_
  137.9 0.9 collective-permute-done.6.refs_6_
  138.8 0.4 collective-permute-done.5.refs_5_
  139.1 1.7 %place_shares.2.refs_3_ = f32[1024,1024]{1,0:T(8,128)} custom-call(s32[1]{0:T(128)} %bitcast.1.refs_0_, bf16[128,1024]{1,0:T(8,128)(2,1)S(1)} %level_two.1.refs_1_, bf16[128,1024]{1,0:T(8,128)(2,1)S(1)} %collective-permute-done.2.refs_2_, bf16[128,1024]{1,0:T(8,128)(2,1)S(1)} %collective-permute-done.3.refs_3_, ...), custom_call_target="tpu_custom_call" | custom-call | tf_op jit(solution)/shard_map/place_shares/pallas_call | solution.py:319
  140.9 0.0 collective-permute-done.1.refs_2_
  140.9 1.0 place_shares.3
Async XLA Ops:
  0.6 46.2 %copy-start = (f32[1024,1024]{1,0:T(8,128)S(1)}, f32[1024,1024]{1,0:T(8,128)}, u32[]{:S(2)}) copy-start(f32[1024,1024]{1,0:T(8,128)} %refs_2_.3) | copy-start | bytes 12582916
  121.9 15.4 %collective-permute-start.3 = (bf16[128,1024]{1,0:T(8,128)(2,1)S(1)}, bf16[128,1024]{1,0:T(8,128)(2,1)S(1)}, u32[]{:S(2)}, u32[]{:S(2)}) collective-permute-start(bf16[128,1024]{1,0:T(8,128)(2,1)S(1)} %level_two.1.refs_1_), channel_id=1, source_target_pairs={{0,32},{16,48},{32,64},{48,80},{64,96},{80,112},{96,0},{112,16},{1... | collective-permute-start | bytes 786440 | tf_op jit(solution)/shard_map/ppermute | solution.py:334
  122.8 14.4 %collective-permute-start.2 = (bf16[128,1024]{1,0:T(8,128)(2,1)S(1)}, bf16[128,1024]{1,0:T(8,128)(2,1)S(1)}, u32[]{:S(2)}, u32[]{:S(2)}) collective-permute-start(bf16[128,1024]{1,0:T(8,128)(2,1)S(1)} %level_two.1.refs_1_), channel_id=1, source_target_pairs={{0,64},{16,80},{32,96},{48,112},{64,0},{80,16},{96,32},{112,48},{1... | collective-permute-start | bytes 786440 | tf_op jit(solution)/shard_map/ppermute | solution.py:334
  125.6 12.2 %collective-permute-start = (bf16[128,1024]{1,0:T(8,128)(2,1)S(1)}, bf16[128,1024]{1,0:T(8,128)(2,1)S(1)}, u32[]{:S(2)}, u32[]{:S(2)}) collective-permute-start(bf16[128,1024]{1,0:T(8,128)(2,1)S(1)} %level_two.1.refs_1_), channel_id=1, source_target_pairs={{0,96},{16,112},{32,0},{48,16},{64,32},{80,48},{96,64},{112,80},{1... | collective-permute-start | bytes 786440 | tf_op jit(solution)/shard_map/ppermute | solution.py:334
  126.8 11.0 %collective-permute-start.4 = (bf16[128,1024]{1,0:T(8,128)(2,1)S(1)}, bf16[128,1024]{1,0:T(8,128)(2,1)S(1)}, u32[]{:S(2)}, u32[]{:S(2)}) collective-permute-start(bf16[128,1024]{1,0:T(8,128)(2,1)S(1)} %level_two.1.refs_1_), channel_id=1, source_target_pairs={{0,16},{16,0},{32,48},{48,32},{64,80},{80,64},{96,112},{112,96},{1... | collective-permute-start | bytes 786440 | tf_op jit(solution)/shard_map/ppermute | solution.py:336
  137.2 1.5 %collective-permute-start.6 = (bf16[128,1024]{1,0:T(8,128)(2,1)S(1)}, bf16[128,1024]{1,0:T(8,128)(2,1)S(1)}, u32[]{:S(2)}, u32[]{:S(2)}) collective-permute-start(bf16[128,1024]{1,0:T(8,128)(2,1)S(1)} %collective-permute-done.3.refs_3_), channel_id=1, source_target_pairs={{0,16},{16,0},{32,48},{48,32},{64,80},{80,64},{96,112},{112,96},{1... | collective-permute-start | bytes 786440 | tf_op jit(solution)/shard_map/ppermute | solution.py:336
  137.2 1.9 %collective-permute-start.5 = (bf16[128,1024]{1,0:T(8,128)(2,1)S(1)}, bf16[128,1024]{1,0:T(8,128)(2,1)S(1)}, u32[]{:S(2)}, u32[]{:S(2)}) collective-permute-start(bf16[128,1024]{1,0:T(8,128)(2,1)S(1)} %collective-permute-done.2.refs_2_), channel_id=1, source_target_pairs={{0,16},{16,0},{32,48},{48,32},{64,80},{80,64},{96,112},{112,96},{1... | collective-permute-start | bytes 786440 | tf_op jit(solution)/shard_map/ppermute | solution.py:336
  137.9 3.0 %collective-permute-start.1 = (bf16[128,1024]{1,0:T(8,128)(2,1)S(1)}, bf16[128,1024]{1,0:T(8,128)(2,1)S(1)}, u32[]{:S(2)}, u32[]{:S(2)}) collective-permute-start(bf16[128,1024]{1,0:T(8,128)(2,1)S(1)} %collective-permute-done.refs_1_), channel_id=1, source_target_pairs={{0,16},{16,0},{32,48},{48,32},{64,80},{80,64},{96,112},{112,96},{1... | collective-permute-start | bytes 786440 | tf_op jit(solution)/shard_map/ppermute | solution.py:336

commit v2 on v1

--- a/solution.py
+++ b/solution.py
@@ -12,6 +12,9 @@
 DIGIT = 32
 F32 = jnp.float32
 BF16 = jnp.bfloat16
+GATHER_STEP = 128
+PACK_STEP = 256
+TWO_STEP = 256
 TURNS = (2, 1, 3)
 PACK_MIB = 16
 ONE_MIB = 36
@@ -108,24 +111,23 @@
 
 
 def lloyd_one_kernel(
-    iters, index_ref, got_ref, centers_ref, slot_ref, coarse_hbm, out_hbm, send_ref, two_ref, share_ref, out_ref, scaled_ref, member_ref, sems
+    iters, index_ref, got_ref, centers_ref, slot_ref, coarse_hbm, out_ref, send_ref, two_ref, share_ref, scaled_ref, member_ref, sem
 ):
     share = share_ref.shape[0]
     start = pl.multiple_of(index_ref[0] * share, share)
-    share_copy = pltpu.make_async_copy(coarse_hbm.at[pl.ds(start, share)], share_ref, sems.at[0])
+    share_copy = pltpu.make_async_copy(coarse_hbm.at[pl.ds(start, share)], share_ref, sem)
     share_copy.start()
     owned, width = centers_ref.shape
     group = CAP * iters
     total = got_ref.shape[0]
     half = total // 2
-    step = 128
-    member_two(group, got_ref, two_ref)
+    step = GATHER_STEP
     low = iota((step, EXTRA), 0) % 8 < CAP
     wide_low = iota((step, width), 0) % 8 < CAP
     for t in range(iters):
         old_ref = centers_ref if t == 0 else out_ref
         rounded = old_ref[...].astype(BF16)
-        mass = jnp.zeros((owned, EXTRA), F32)
+        mass = jnp.zeros((1, owned), F32)
         for c in range(0, half, step):
             def rows(lo, hi, keep):
                 got = got_ref[2 * c : 2 * (c + step), lo:hi].astype(F32).reshape(step // 8, 16, hi - lo)
@@ -138,37 +140,33 @@
             extra = rows(width, width + EXTRA, low)
             values = rows(0, width, wide_low)
             label = ((extra[:, 0:1] - 1.0) * DIGIT + extra[:, 1:2]).astype(jnp.int32)
-            member = onehot(iota((step, owned), 1) == label)
+            mask = iota((step, owned), 1) == label
+            member = onehot(mask)
             member_ref[c : c + step, :] = member
             nearest = nn(member, rounded)
             distance = jnp.sum((values - nearest) ** 2, axis=1, keepdims=True) / width
             weights = 1.0 / (1.0 + distance)
-            scaled_ref[c : c + step, :width] = (weights * values).astype(BF16)
-            scaled_ref[c : c + step, width:] = weight_columns(weights)
-        member = member_ref[...]
-        mass = tn(member, scaled_ref[:, width:])
-        scale = 1.0 / (jnp.sum(mass, axis=1, keepdims=True) + 1.0)
-        out_ref[...] = (tn(member, scaled_ref[:, :width]) + old_ref[...]) * scale
-    out_copy = pltpu.make_async_copy(out_ref, out_hbm, sems.at[1])
-    out_copy.start()
+            scaled_ref[c : c + step, :] = (weights * values).astype(BF16)
+            mass = mass + jnp.sum(jnp.where(mask, weights, 0.0), axis=0, keepdims=True)
+        scale = 1.0 / (as_column(mass) + 1.0)
+        out_ref[...] = (tn(member_ref[...], scaled_ref[...]) + old_ref[...]) * scale
     rounded = out_ref[...].astype(BF16)
     slots = send_ref.shape[0]
-    step = 256
+    step = PACK_STEP
     for s in range(0, slots, step):
         pick = onehot(iota((step, owned), 0) + s == slot_ref[...])
         send_ref[s : s + step, :] = nn(pick, rounded).astype(BF16)
+    member_two(group, got_ref, two_ref)
     share_copy.wait()
-    out_copy.wait()
-
-
-def weight_columns(weights):
-    n = weights.shape[0]
-    hi = weights.astype(BF16).astype(F32)
-    mid = (weights - hi).astype(BF16).astype(F32)
-    low = weights - hi - mid
-    lane = iota((n, 128), 1)
-    cols = jnp.where(lane == 0, hi, jnp.where(lane == 1, mid, jnp.where(lane == 2, low, 0.0)))
-    return cols.astype(BF16)
+
+
+def as_column(row):
+    step = 128
+    diagonal = iota((step, step), 0) == iota((step, step), 1)
+    parts = [
+        jnp.sum(jnp.where(diagonal, row[:, c : c + step], 0.0), axis=1, keepdims=True) for c in range(0, row.shape[1], step)
+    ]
+    return jnp.concatenate(parts, axis=0)
 
 
 def member_two(group, got_ref, member_ref):
@@ -187,7 +185,7 @@
 def lloyd_two_kernel(got_ref, member_ref, centers_ref, out_ref, norm_ref, weighted_ref):
     share, width = centers_ref.shape
     total = got_ref.shape[0]
-    step = 256
+    step = TWO_STEP
     centers = centers_ref[...]
     diagonal = iota((share, share), 0) == iota((share, share), 1)
     for t in range(ITER2):
@@ -195,6 +193,7 @@
         both = jnp.concatenate([hi, lo], axis=0)
         squares = jnp.sum(centers * centers, axis=1, keepdims=True)
         squares = jnp.sum(jnp.where(diagonal, squares, 0.0), axis=0, keepdims=True)
+        mass = jnp.zeros((1, share), F32)
         for c in range(0, total, step):
             rows = got_ref[c : c + step, :]
             member = member_ref[c : c + step, :].astype(F32)
@@ -206,13 +205,12 @@
             rest = jnp.sum(member * (squares - 2.0 * cross), axis=1, keepdims=True)
             distance = jnp.maximum(norm_ref[c : c + step, :] + rest, 0.0) / width
             weights = member / (1.0 + distance)
+            mass = mass + jnp.sum(weights, axis=0, keepdims=True)
             hi, lo = split2(weights)
             weighted_ref[c : c + step, :share] = hi
             weighted_ref[c : c + step, share:] = lo
-        weighted = weighted_ref[...]
-        sums = tn(weighted, got_ref[...])
-        mass = tn(weighted, jnp.ones((total, 128), BF16))
-        scale = 1.0 / (mass[:share, :1] + mass[share:, :1] + 1.0)
+        sums = tn(weighted_ref[...], got_ref[...])
+        scale = 1.0 / (as_column(mass) + 1.0)
         centers = (sums[:share] + sums[share:] + centers) * scale
     out_ref[...] = centers.astype(BF16)
 
@@ -231,6 +229,14 @@
         copies[-1].start()
     for copy in copies:
         copy.wait()
+
+
+def place_first_kernel(places, groups, index_ref, fine_ref, *refs):
+    fine_hbm, fine_sem = refs[len(places)], refs[-1]
+    fine_copy = pltpu.make_async_copy(fine_ref, fine_hbm, fine_sem)
+    fine_copy.start()
+    place_kernel(places, groups, index_ref, *refs[: len(places)], *refs[len(places) + 1 : -1])
+    fine_copy.wait()
 
 
 def whole():
@@ -277,18 +283,17 @@
     return pl.pallas_call(
         lambda *refs: lloyd_one_kernel(iters, *refs),
         out_shape=(
-            pltpu.HBM((owned, width), F32),
+            pltpu.VMEM((owned, width), F32),
             jax.ShapeDtypeStruct((slots_two, width), BF16),
             jax.ShapeDtypeStruct((slots_two, share), BF16),
             jax.ShapeDtypeStruct((share, width), F32),
         ),
         in_specs=[pl.BlockSpec(memory_space=pltpu.SMEM)] + [whole()] * 3 + [in_hbm()],
-        out_specs=(in_hbm(), whole(), whole(), whole()),
+        out_specs=(whole(),) * 4,
         scratch_shapes=[
-            pltpu.VMEM((owned, width), F32),
-            pltpu.VMEM((half, width + EXTRA), BF16),
+            pltpu.VMEM((half, width), BF16),
             pltpu.VMEM((half, owned), BF16),
-            pltpu.SemaphoreType.DMA((2,)),
+            pltpu.SemaphoreType.DMA,
         ],
         compiler_params=params(ONE_MIB),
         name="level_one",
@@ -312,31 +317,45 @@
     )(got, member, centers)
 
 
-def place(groups, index, blocks, out=None):
+def place(groups, index, blocks, out=None, fine=None):
     places, arrays = list(blocks), list(blocks.values())
     share, width = arrays[0].shape
-    extra = [] if out is None else [out]
+    kernel, before, after = place_kernel, [], [out]
+    out_shape, out_specs = pltpu.HBM((groups * share, width), F32), in_hbm()
+    scratch = [pltpu.VMEM((len(arrays), share, width), F32), pltpu.SemaphoreType.DMA((len(arrays),))]
+    if out is None:
+        kernel, before, after = place_first_kernel, [fine], []
+        out_shape, out_specs = (pltpu.HBM(fine.shape, F32), out_shape), (in_hbm(), in_hbm())
+        scratch.append(pltpu.SemaphoreType.DMA)
     return pl.pallas_call(
-        lambda *refs: place_kernel(places, groups, *refs),
-        out_shape=pltpu.HBM((groups * share, width), F32),
-        in_specs=[pl.BlockSpec(memory_space=pltpu.SMEM)] + [whole()] * len(arrays) + [in_hbm()] * len(extra),
-        out_specs=in_hbm(),
-        scratch_shapes=[pltpu.VMEM((len(arrays), share, width), F32), pltpu.SemaphoreType.DMA((len(arrays),))],
-        input_output_aliases={1 + len(arrays): 0} if extra else {},
+        lambda *refs: kernel(places, groups, *refs),
+        out_shape=out_shape,
+        in_specs=[pl.BlockSpec(memory_space=pltpu.SMEM)]
+        + [whole()] * (len(before) + len(arrays))
+        + [in_hbm()] * len(after),
+        out_specs=out_specs,
+        scratch_shapes=scratch,
+        input_output_aliases={1 + len(arrays): 0} if after else {},
         compiler_params=params(PLACE_MIB),
+        cost_estimate=pl.CostEstimate(
+            flops=len(arrays) * share * width, bytes_accessed=len(arrays) * share * width * 6, transcendentals=0
+        ),
         name="place_shares",
-    )(index, *arrays, *extra)
-
-
-def gather_shares(own, groups, index):
-    blocks = {(0, 0): own}
-    for k in TURNS:
-        blocks[(k, 0)] = lax.ppermute(own, "grp", [(g, (g + 2 * k) % groups) for g in range(groups)])
-    for k in (0, *TURNS):
-        blocks[(k, 1)] = lax.ppermute(blocks[(k, 0)], "grp", [(g, g ^ 1) for g in range(groups)])
-    last = TURNS[-1]
-    out = place(groups, index, {p: b for p, b in blocks.items() if p[0] != last})
-    return place(groups, index, {p: b for p, b in blocks.items() if p[0] == last}, out)
+    )(index, *before, *arrays, *after)
+
+
+def gather_shares(own, groups, index, fine):
+    def other_core(rows):
+        return lax.ppermute(rows, "grp", [(g, g ^ 1) for g in range(groups)])
+
+    far = [lax.ppermute(own, "grp", [(g, (g + 2 * k) % groups) for g in range(groups)]) for k in TURNS]
+    fine, out = place(groups, index, {(0, 0): own}, fine=fine)
+    out, own = lax.optimization_barrier((out, own))
+    blocks = {(0, 1): other_core(own)}
+    for k, rows in zip(TURNS, far):
+        out, rows = lax.optimization_barrier((out, rows))
+        blocks |= {(k, 0): rows, (k, 1): other_core(rows)}
+    return fine, place(groups, index, blocks, out)
 
 
 def shards(points, fine_initial, coarse_initial, assign, parent):
@@ -362,7 +381,7 @@
         send_two.reshape(devices, CAP_SHARE, width), ("grp", "sub"), split_axis=0, concat_axis=0, tiled=True
     ).reshape(slots_two, width)
     own = level_two(got_two, member, centers)
-    return fine, gather_shares(own, groups, me)
+    return gather_shares(own, groups, me, fine)
 
 
 def solution(mesh):

time: 143 us -> 141 us (0.986)
  waiting for transfers between devices: 11.8 us -> 9.58 us
    ppermute x3, waiting for transfers between devices: 10.5 us -> 7.82 us  [gather_shares(): lax.ppermute(own, 'grp', [(g, (g + 2 * k) % groups) for g in range(groups)])]
  transfers between devices with their start and end apart: 7 -> 7, of which waited for: 4 -> 5; matrix products, arithmetic and copies ran while one was open for 0% -> 0% of each run, Pallas kernels for 1% -> 2%
where the time goes in v2:
time: 141 us; the launch traced here: 140 us
  blocking collectives  99.1 us (70%)
  Pallas kernels  23.9 us (17%)
  waiting for transfers between devices  9.58 us (7%)
  starting transfers between devices  6.19 us (4%)
    all_to_all x1, blocking collectives, shards(): lax.all_to_all(send_two.reshape(devices, CAP_SHARE, width), ('grp', 'sub'...  55.8 us
    all_to_all x1, blocking collectives, shards(): lax.all_to_all(send.reshape(devices, CAP * iters, width + EXTRA), ('grp',...  43.3 us
    pallas_call x1, Pallas kernels, level_one(): pl.pallas_call(lambda *refs: lloyd_one_kernel(iters, *refs), out_shape=(p...  11.4 us
    ppermute x3, waiting for transfers between devices, gather_shares(): lax.ppermute(own, 'grp', [(g, (g + 2 * k) % groups) for g in range(groups)])  7.82 us
    ppermute x3, starting transfers between devices, gather_shares(): lax.ppermute(own, 'grp', [(g, (g + 2 * k) % groups) for g in range(groups)])  5.58 us
    pallas_call x1, Pallas kernels, level_two(): pl.pallas_call(lloyd_two_kernel, out_shape=jax.ShapeDtypeStruct((share, w...  5.54 us
    pallas_call x2, Pallas kernels, place(): pl.pallas_call(lambda *refs: kernel(places, groups, *refs), out_shape=out...  4.11 us
    pallas_call x1, Pallas kernels, pack_points(): pl.pallas_call(lambda *refs: pack_one_kernel(devices, owned, share, subs,...  2.91 us
  transfers between devices with their start and end apart: 7, of which 5 were waited for; matrix products, arithmetic and copies ran while one was open for 0% of the time, Pallas kernels for 2%

profile of v2, /device:TPU:0, one launch (start us, length us, event | category | flops | bytes accessed | tf_op | source)
XLA Modules:
  0.0 139.7 jit_solution(1608952720071499462)
XLA Ops:
  0.6 0.0 copy-start
  0.6 2.9 %pack_points.1 = (bf16[1024,1152]{1,0:T(8,128)(2,1)S(1)}, s32[1,1024]{1,0:T(1,128)S(1)}) custom-call(s32[2,256]{1,0:T(2,128)} %refs_0_.1, s32[1,1024]{1,0:T(1,128)} %bitcast.10, bf16[256,1024]{1,0:T(8,128)(2,1)} %refs_2_.2), custom_call_target="tpu_custom_call" | custom-call | tf_op jit(solution)/shard_map/pack_points/pallas_call | solution.py:260
  3.6 43.3 %all_to_all.10 = bf16[128,8,1152]{2,1,0:T(8,128)(2,1)S(1)} all-to-all(bf16[128,8,1152]{2,1,0:T(8,128)(2,1)S(1)} %bitcast.9), channel_id=1, replica_groups=mesh['grp'=8,'sub'=16] {'grp','sub'}, dimensions={0} | all-to-all | bytes 4718592 | tf_op jit(solution)/shard_map/all_to_all | solution.py:374
  46.9 0.0 copy-done
  46.9 11.4 %level_one.1 = (f32[1024,1024]{1,0:T(8,128)S(1)}, bf16[2048,1024]{1,0:T(8,128)(2,1)S(1)}, bf16[2048,128]{1,0:T(8,128)(2,1)S(1)}, f32[128,1024]{1,0:T(8,128)S(1)}) custom-call(s32[1]{0:T(128)} %bitcast.1.refs_0_, bf16[1024,1152]{1,0:T(8,128)(2,1)S(1)} %bitcast.7, f32[1024,1024]{1,0:T(8,128)S(1)} %copy-done, s32[1,1024]{1,0:T(1,128)S(1)} %get-tuple-element.23.refs_3_, ...), custom_call_target="tpu_custom_call" | custom-call | tf_op jit(solution)/shard_map/level_one/pallas_call | solution.py:283
  58.2 55.8 %all_to_all.11 = bf16[128,16,1024]{2,1,0:T(8,128)(2,1)S(1)} all-to-all(bf16[128,16,1024]{2,1,0:T(8,128)(2,1)S(1)} %bitcast.8), channel_id=1, replica_groups=mesh['grp'=8,'sub'=16] {'grp','sub'}, dimensions={0} | all-to-all | bytes 8388608 | tf_op jit(solution)/shard_map/all_to_all | solution.py:380
  114.1 5.5 %level_two.1.refs_2_ = bf16[128,1024]{1,0:T(8,128)(2,1)S(1)} custom-call(bf16[2048,1024]{1,0:T(8,128)(2,1)S(1)} %bitcast.6, bf16[2048,128]{1,0:T(8,128)(2,1)S(1)} %get-tuple-element.26.member_ref, f32[128,1024]{1,0:T(8,128)S(1)} %get-tuple-element.27.centers_ref), custom_call_target="tpu_custom_call" | custom-call | tf_op jit(solution)/shard_map/level_two/pallas_call | solution.py:306
  119.6 2.3 %collective-permute-start.1 = (bf16[128,1024]{1,0:T(8,128)(2,1)S(1)}, bf16[128,1024]{1,0:T(8,128)(2,1)S(1)}, u32[]{:S(2)}, u32[]{:S(2)}) collective-permute-start(bf16[128,1024]{1,0:T(8,128)(2,1)S(1)} %level_two.1.refs_2_), channel_id=1, source_target_pairs={{0,64},{16,80},{32,96},{48,112},{64,0},{80,16},{96,32},{112,48},{1... | collective-permute-start | bytes 786440 | tf_op jit(solution)/shard_map/ppermute | solution.py:351
  122.0 0.8 collective-permute-start.3
  122.8 2.4 %collective-permute-start.5 = (bf16[128,1024]{1,0:T(8,128)(2,1)S(1)}, bf16[128,1024]{1,0:T(8,128)(2,1)S(1)}, u32[]{:S(2)}, u32[]{:S(2)}) collective-permute-start(bf16[128,1024]{1,0:T(8,128)(2,1)S(1)} %level_two.1.refs_2_), channel_id=1, source_target_pairs={{0,96},{16,112},{32,0},{48,16},{64,32},{80,48},{96,64},{112,80},{1... | collective-permute-start | bytes 786440 | tf_op jit(solution)/shard_map/ppermute | solution.py:351
  125.2 2.2 %place_shares.2 = (f32[1024,1024]{1,0:T(8,128)}, f32[1024,1024]{1,0:T(8,128)}) custom-call(s32[1]{0:T(128)} %bitcast.1.refs_0_, f32[1024,1024]{1,0:T(8,128)S(1)} %get-tuple-element.24.refs_1_, bf16[128,1024]{1,0:T(8,128)(2,1)S(1)} %level_two.1.refs_2_), custom_call_target="tpu_custom_call" | custom-call | flops 131072 | bytes 786432 | tf_op jit(solution)/shard_map/place_shares/pallas_call | solution.py:330
  127.4 0.1 collective-permute-start
  127.5 2.9 %collective-permute-done.1.refs_2_ = bf16[128,1024]{1,0:T(8,128)(2,1)S(1)} collective-permute-done((bf16[128,1024]{1,0:T(8,128)(2,1)S(1)}, bf16[128,1024]{1,0:T(8,128)(2,1)S(1)}, u32[]{:S(2)}, u32[]{:S(2)}) %collective-permute-start.1) | collective-permute-done | bytes 262176 | tf_op jit(solution)/shard_map/ppermute | solution.py:351
  130.4 4.9 %collective-permute-done.3.refs_4_ = bf16[128,1024]{1,0:T(8,128)(2,1)S(1)} collective-permute-done((bf16[128,1024]{1,0:T(8,128)(2,1)S(1)}, bf16[128,1024]{1,0:T(8,128)(2,1)S(1)}, u32[]{:S(2)}, u32[]{:S(2)}) %collective-permute-start.3) | collective-permute-done | bytes 262176 | tf_op jit(solution)/shard_map/ppermute | solution.py:351
  135.3 0.0 collective-permute-done.5.refs_6_
  135.3 0.0 collective-permute-start.6
  135.3 0.5 collective-permute-start.4
  135.8 0.0 collective-permute-start.2
  135.9 0.0 collective-permute-done.refs_1_
  135.9 1.0 collective-permute-done.6.refs_7_
  136.9 0.4 collective-permute-done.4.refs_5_
  137.2 0.4 collective-permute-done.2.refs_3_
  137.6 1.9 %place_shares.3 = f32[1024,1024]{1,0:T(8,128)} custom-call(s32[1]{0:T(128)} %bitcast.1.refs_0_, bf16[128,1024]{1,0:T(8,128)(2,1)S(1)} %collective-permute-done.refs_1_, bf16[128,1024]{1,0:T(8,128)(2,1)S(1)} %collective-permute-done.1.refs_2_, bf16[128,1024]{1,0:T(8,128)(2,1)S(1)} %collective-permute-done.2.refs_3_, ...), custom_call_target="tpu_custom_call", output_to_operand_aliasing={{}: (8, {})} | custom-call | flops 917504 | bytes 5505024 | tf_op jit(solution)/shard_map/place_shares/pallas_call | solution.py:330
Async XLA Ops:
  0.6 46.2 %copy-start = (f32[1024,1024]{1,0:T(8,128)S(1)}, f32[1024,1024]{1,0:T(8,128)}, u32[]{:S(2)}) copy-start(f32[1024,1024]{1,0:T(8,128)} %refs_2_.3) | copy-start | bytes 12582916
  119.6 10.8 %collective-permute-start.1 = (bf16[128,1024]{1,0:T(8,128)(2,1)S(1)}, bf16[128,1024]{1,0:T(8,128)(2,1)S(1)}, u32[]{:S(2)}, u32[]{:S(2)}) collective-permute-start(bf16[128,1024]{1,0:T(8,128)(2,1)S(1)} %level_two.1.refs_2_), channel_id=1, source_target_pairs={{0,64},{16,80},{32,96},{48,112},{64,0},{80,16},{96,32},{112,48},{1... | collective-permute-start | bytes 786440 | tf_op jit(solution)/shard_map/ppermute | solution.py:351
  122.0 13.3 %collective-permute-start.3 = (bf16[128,1024]{1,0:T(8,128)(2,1)S(1)}, bf16[128,1024]{1,0:T(8,128)(2,1)S(1)}, u32[]{:S(2)}, u32[]{:S(2)}) collective-permute-start(bf16[128,1024]{1,0:T(8,128)(2,1)S(1)} %level_two.1.refs_2_), channel_id=1, source_target_pairs={{0,32},{16,48},{32,64},{48,80},{64,96},{80,112},{96,0},{112,16},{1... | collective-permute-start | bytes 786440 | tf_op jit(solution)/shard_map/ppermute | solution.py:351
  122.8 12.5 %collective-permute-start.5 = (bf16[128,1024]{1,0:T(8,128)(2,1)S(1)}, bf16[128,1024]{1,0:T(8,128)(2,1)S(1)}, u32[]{:S(2)}, u32[]{:S(2)}) collective-permute-start(bf16[128,1024]{1,0:T(8,128)(2,1)S(1)} %level_two.1.refs_2_), channel_id=1, source_target_pairs={{0,96},{16,112},{32,0},{48,16},{64,32},{80,48},{96,64},{112,80},{1... | collective-permute-start | bytes 786440 | tf_op jit(solution)/shard_map/ppermute | solution.py:351
  127.4 8.4 %collective-permute-start = (bf16[128,1024]{1,0:T(8,128)(2,1)S(1)}, bf16[128,1024]{1,0:T(8,128)(2,1)S(1)}, u32[]{:S(2)}, u32[]{:S(2)}) collective-permute-start(bf16[128,1024]{1,0:T(8,128)(2,1)S(1)} %level_two.1.refs_2_), channel_id=1, source_target_pairs={{0,16},{16,0},{32,48},{48,32},{64,80},{80,64},{96,112},{112,96},{1... | collective-permute-start | bytes 786440 | tf_op jit(solution)/shard_map/ppermute | solution.py:349
  135.3 1.5 %collective-permute-start.6 = (bf16[128,1024]{1,0:T(8,128)(2,1)S(1)}, bf16[128,1024]{1,0:T(8,128)(2,1)S(1)}, u32[]{:S(2)}, u32[]{:S(2)}) collective-permute-start(bf16[128,1024]{1,0:T(8,128)(2,1)S(1)} %collective-permute-done.5.refs_6_), channel_id=1, source_target_pairs={{0,16},{16,0},{32,48},{48,32},{64,80},{80,64},{96,112},{112,96},{1... | collective-permute-start | bytes 786440 | tf_op jit(solution)/shard_map/ppermute | solution.py:349
  135.3 1.9 %collective-permute-start.4 = (bf16[128,1024]{1,0:T(8,128)(2,1)S(1)}, bf16[128,1024]{1,0:T(8,128)(2,1)S(1)}, u32[]{:S(2)}, u32[]{:S(2)}) collective-permute-start(bf16[128,1024]{1,0:T(8,128)(2,1)S(1)} %collective-permute-done.3.refs_4_), channel_id=1, source_target_pairs={{0,16},{16,0},{32,48},{48,32},{64,80},{80,64},{96,112},{112,96},{1... | collective-permute-start | bytes 786440 | tf_op jit(solution)/shard_map/ppermute | solution.py:349
  135.8 1.8 %collective-permute-start.2 = (bf16[128,1024]{1,0:T(8,128)(2,1)S(1)}, bf16[128,1024]{1,0:T(8,128)(2,1)S(1)}, u32[]{:S(2)}, u32[]{:S(2)}) collective-permute-start(bf16[128,1024]{1,0:T(8,128)(2,1)S(1)} %collective-permute-done.1.refs_2_), channel_id=1, source_target_pairs={{0,16},{16,0},{32,48},{48,32},{64,80},{80,64},{96,112},{112,96},{1... | collective-permute-start | bytes 786440 | tf_op jit(solution)/shard_map/ppermute | solution.py:349

commit v3 on v2

--- a/solution.py
+++ b/solution.py
@@ -73,12 +73,12 @@
     ]
     for copy in copies:
         copy.start()
+    iters, n = assign_ref.shape
+    slots = devices * CAP
+    width = points_ref.shape[1]
+
+    spread = onehot(iota((slots, devices), 0) == iota((slots, devices), 1) * CAP)
     copies[0].wait()
-    iters, n = assign_ref.shape
-    group = CAP * iters
-    slots = devices * group
-    width = points_ref.shape[1]
-
     parent = parent_ref[...]
     k = parent.shape[1]
     per_sub = share * (devices // subs)
@@ -89,25 +89,24 @@
     lane = iota((EXTRA, k), 0)
     labels = jnp.where(lane == CAP_SHARE + rank, parent % share + 1, 0)
     labels = nt(onehot(member), labels.astype(F32).astype(BF16)).astype(BF16)
-    spread = onehot(iota((slots, devices), 0) == iota((slots, devices), 1) * group)
     extra = nn(spread, labels)
 
     copies[1].wait()
-    hot = None
     slot_iota = iota((slots, n), 0)
     for t in range(iters):
         target = assign_ref[t : t + 1, :]
         dest = target // owned
         local = target % owned
         rank = rank_in_bucket(iota((devices, n), 0) == dest)
-        mask = slot_iota == dest * group + t * CAP + rank
-        hot = mask if hot is None else jnp.logical_or(hot, mask)
-        lane = iota((EXTRA, n), 0)
+        hot = onehot(slot_iota == dest * CAP + rank)
+        lane = iota((EXTRA, n), 0) - 2 * t
         digits = jnp.where(lane == 0, local // DIGIT + 1, jnp.where(lane == 1, local % DIGIT, 0))
-        extra = extra + nt(onehot(mask), digits.astype(F32).astype(BF16))
-    out_ref[:, width:] = extra.astype(BF16)
-    copies[2].wait()
-    out_ref[:, :width] = nn(onehot(hot), points_ref[...]).astype(BF16)
+        extra = extra + nt(hot, digits.astype(F32).astype(BF16))
+        if t == 0:
+            copies[2].wait()
+        rows = nn(hot, points_ref[...]).reshape(devices, CAP, width)
+        out_ref[:, :, t * width : (t + 1) * width] = rows.astype(BF16)
+    out_ref[:, :, iters * width :] = extra.reshape(devices, CAP, EXTRA).astype(BF16)
 
 
 def lloyd_one_kernel(
@@ -118,28 +117,20 @@
     share_copy = pltpu.make_async_copy(coarse_hbm.at[pl.ds(start, share)], share_ref, sem)
     share_copy.start()
     owned, width = centers_ref.shape
-    group = CAP * iters
-    total = got_ref.shape[0]
-    half = total // 2
+    half = got_ref.shape[0] * CAP
     step = GATHER_STEP
-    low = iota((step, EXTRA), 0) % 8 < CAP
-    wide_low = iota((step, width), 0) % 8 < CAP
     for t in range(iters):
         old_ref = centers_ref if t == 0 else out_ref
         rounded = old_ref[...].astype(BF16)
         mass = jnp.zeros((1, owned), F32)
         for c in range(0, half, step):
-            def rows(lo, hi, keep):
-                got = got_ref[2 * c : 2 * (c + step), lo:hi].astype(F32).reshape(step // 8, 16, hi - lo)
-                even = got[:, 0:8, :].reshape(step, hi - lo)
-                odd = got[:, 8:16, :].reshape(step, hi - lo)
-                if t == 0:
-                    return jnp.where(keep, even, pltpu.roll(odd, CAP, 0))
-                return jnp.where(keep, pltpu.roll(even, step - CAP, 0), odd)
-
-            extra = rows(width, width + EXTRA, low)
-            values = rows(0, width, wide_low)
-            label = ((extra[:, 0:1] - 1.0) * DIGIT + extra[:, 1:2]).astype(jnp.int32)
+            def rows(lo, size):
+                got = got_ref[c // CAP : (c + step) // CAP, :, lo : lo + size]
+                return got.astype(F32).reshape(step, size)
+
+            extra = rows(iters * width, EXTRA)
+            values = rows(t * width, width)
+            label = ((extra[:, 2 * t : 2 * t + 1] - 1.0) * DIGIT + extra[:, 2 * t + 1 : 2 * t + 2]).astype(jnp.int32)
             mask = iota((step, owned), 1) == label
             member = onehot(mask)
             member_ref[c : c + step, :] = member
@@ -156,7 +147,7 @@
     for s in range(0, slots, step):
         pick = onehot(iota((step, owned), 0) + s == slot_ref[...])
         send_ref[s : s + step, :] = nn(pick, rounded).astype(BF16)
-    member_two(group, got_ref, two_ref)
+    member_two(got_ref, two_ref)
     share_copy.wait()
 
 
@@ -169,12 +160,13 @@
     return jnp.concatenate(parts, axis=0)
 
 
-def member_two(group, got_ref, member_ref):
+def member_two(got_ref, member_ref):
     total, share = member_ref.shape
-    slots = got_ref.shape[0]
-    devices = slots // group
-    first = onehot(iota((devices, slots), 1) == iota((devices, slots), 0) * group)
-    labels = nn(first, got_ref[:, got_ref.shape[1] - EXTRA :]).astype(BF16)
+    devices = got_ref.shape[0]
+    slots = devices * CAP
+    first = onehot(iota((devices, slots), 1) == iota((devices, slots), 0) * CAP)
+    extra = got_ref[:, :, got_ref.shape[2] - EXTRA :].astype(F32).reshape(slots, EXTRA)
+    labels = nn(first, extra.astype(BF16)).astype(BF16)
     expand = onehot(iota((total, devices), 0) // CAP_SHARE == iota((total, devices), 1))
     labels = nn(expand, labels)
     mine = iota((total, EXTRA), 1) == CAP_SHARE + iota((total, EXTRA), 0) % CAP_SHARE
@@ -260,7 +252,7 @@
     return pl.pallas_call(
         lambda *refs: pack_one_kernel(devices, owned, share, subs, *refs),
         out_shape=(
-            jax.ShapeDtypeStruct((devices * CAP * iters, points.shape[1] + EXTRA), BF16),
+            jax.ShapeDtypeStruct((devices, CAP, iters * points.shape[1] + EXTRA), BF16),
             jax.ShapeDtypeStruct(parent.shape, jnp.int32),
         ),
         in_specs=[in_hbm()] * 3,
@@ -278,7 +270,7 @@
 
 def level_one(iters, devices, share, index, got, centers, slot_two, coarse):
     owned, width = centers.shape
-    half = got.shape[0] // 2
+    half = devices * CAP
     slots_two = devices * CAP_SHARE
     return pl.pallas_call(
         lambda *refs: lloyd_one_kernel(iters, *refs),
@@ -371,9 +363,7 @@
     me = lax.axis_index("grp").astype(jnp.int32).reshape(1)
     send, slot_two = pack_points(devices, subs, owned, share, assign, parent.reshape(1, owned), points)
     send, me = lax.optimization_barrier((send, me))
-    got = lax.all_to_all(
-        send.reshape(devices, CAP * iters, width + EXTRA), ("grp", "sub"), split_axis=0, concat_axis=0, tiled=True
-    ).reshape(devices * CAP * iters, width + EXTRA)
+    got = lax.all_to_all(send, ("grp", "sub"), split_axis=0, concat_axis=0, tiled=True)
     fine, send_two, member, centers = level_one(
         iters, devices, share, me, got, fine_initial, slot_two, coarse_initial
     )

time: 141 us -> 139 us (0.986)
  no operation moved by 1% of the time
where the time goes in v3:
time: 139 us; the launch traced here: 138 us
  blocking collectives  97.7 us (70%)
  Pallas kernels  23.9 us (17%)
  waiting for transfers between devices  9.57 us (7%)
  starting transfers between devices  6.2 us (4%)
    all_to_all x1, blocking collectives, shards(): lax.all_to_all(send_two.reshape(devices, CAP_SHARE, width), ('grp', 'sub'...  55.7 us
    all_to_all x1, blocking collectives, shards(): lax.all_to_all(send, ('grp', 'sub'), split_axis=0, concat_axis=0, tiled=T...  42 us
    pallas_call x1, Pallas kernels, level_one(): pl.pallas_call(lambda *refs: lloyd_one_kernel(iters, *refs), out_shape=(p...  11.3 us
    ppermute x3, waiting for transfers between devices, gather_shares(): lax.ppermute(own, 'grp', [(g, (g + 2 * k) % groups) for g in range(groups)])  7.81 us
    ppermute x3, starting transfers between devices, gather_shares(): lax.ppermute(own, 'grp', [(g, (g + 2 * k) % groups) for g in range(groups)])  5.59 us
    pallas_call x1, Pallas kernels, level_two(): pl.pallas_call(lloyd_two_kernel, out_shape=jax.ShapeDtypeStruct((share, w...  5.54 us
    pallas_call x2, Pallas kernels, place(): pl.pallas_call(lambda *refs: kernel(places, groups, *refs), out_shape=out...  4.11 us
    pallas_call x1, Pallas kernels, pack_points(): pl.pallas_call(lambda *refs: pack_one_kernel(devices, owned, share, subs,...  2.93 us
  transfers between devices with their start and end apart: 7, of which 5 were waited for; matrix products, arithmetic and copies ran while one was open for 0% of the time, Pallas kernels for 2%

profile of v3, /device:TPU:0, one launch (start us, length us, event | category | flops | bytes accessed | tf_op | source)
XLA Modules:
  0.0 138.2 jit_solution(14326351188337968682)
XLA Ops:
  0.6 0.0 copy-start
  0.6 2.9 %pack_points.1 = (bf16[128,4,2176]{2,1,0:T(4,128)(2,1)S(1)}, s32[1,1024]{1,0:T(1,128)S(1)}) custom-call(s32[2,256]{1,0:T(2,128)} %refs_0_.1, s32[1,1024]{1,0:T(1,128)} %bitcast.6, bf16[256,1024]{1,0:T(8,128)(2,1)} %refs_2_.2), custom_call_target="tpu_custom_call" | custom-call | tf_op jit(solution)/shard_map/pack_points/pallas_call | solution.py:252
  3.6 42.0 %all_to_all.10.refs_1_ = bf16[128,4,2176]{2,1,0:T(4,128)(2,1)S(1)} all-to-all(bf16[128,4,2176]{2,1,0:T(4,128)(2,1)S(1)} %get-tuple-element.22), channel_id=1, replica_groups=mesh['grp'=8,'sub'=16] {'grp','sub'}, dimensions={0} | all-to-all | bytes 4456448 | tf_op jit(solution)/shard_map/all_to_all | solution.py:366
  45.6 0.0 copy-done
  45.6 11.3 %level_one.1 = (f32[1024,1024]{1,0:T(8,128)S(1)}, bf16[2048,1024]{1,0:T(8,128)(2,1)S(1)}, bf16[2048,128]{1,0:T(8,128)(2,1)S(1)}, f32[128,1024]{1,0:T(8,128)S(1)}) custom-call(s32[1]{0:T(128)} %bitcast.1.refs_0_, bf16[128,4,2176]{2,1,0:T(4,128)(2,1)S(1)} %all_to_all.10.refs_1_, f32[1024,1024]{1,0:T(8,128)S(1)} %copy-done, ...), custom_call_target="tpu_custom_call" | custom-call | tf_op jit(solution)/shard_map/level_one/pallas_call | solution.py:275
  56.8 55.7 %all_to_all.11 = bf16[128,16,1024]{2,1,0:T(8,128)(2,1)S(1)} all-to-all(bf16[128,16,1024]{2,1,0:T(8,128)(2,1)S(1)} %bitcast.5), channel_id=1, replica_groups=mesh['grp'=8,'sub'=16] {'grp','sub'}, dimensions={0} | all-to-all | bytes 8388608 | tf_op jit(solution)/shard_map/all_to_all | solution.py:370
  112.6 5.5 %level_two.1.refs_2_ = bf16[128,1024]{1,0:T(8,128)(2,1)S(1)} custom-call(bf16[2048,1024]{1,0:T(8,128)(2,1)S(1)} %bitcast.4, bf16[2048,128]{1,0:T(8,128)(2,1)S(1)} %get-tuple-element.26.member_ref, f32[128,1024]{1,0:T(8,128)S(1)} %get-tuple-element.27.centers_ref), custom_call_target="tpu_custom_call" | custom-call | tf_op jit(solution)/shard_map/level_two/pallas_call | solution.py:298
  118.1 2.4 %collective-permute-start.1 = (bf16[128,1024]{1,0:T(8,128)(2,1)S(1)}, bf16[128,1024]{1,0:T(8,128)(2,1)S(1)}, u32[]{:S(2)}, u32[]{:S(2)}) collective-permute-start(bf16[128,1024]{1,0:T(8,128)(2,1)S(1)} %level_two.1.refs_2_), channel_id=1, source_target_pairs={{0,64},{16,80},{32,96},{48,112},{64,0},{80,16},{96,32},{112,48},{1... | collective-permute-start | bytes 786440 | tf_op jit(solution)/shard_map/ppermute | solution.py:343
  120.5 0.8 collective-permute-start.3
  121.3 2.4 %collective-permute-start.5 = (bf16[128,1024]{1,0:T(8,128)(2,1)S(1)}, bf16[128,1024]{1,0:T(8,128)(2,1)S(1)}, u32[]{:S(2)}, u32[]{:S(2)}) collective-permute-start(bf16[128,1024]{1,0:T(8,128)(2,1)S(1)} %level_two.1.refs_2_), channel_id=1, source_target_pairs={{0,96},{16,112},{32,0},{48,16},{64,32},{80,48},{96,64},{112,80},{1... | collective-permute-start | bytes 786440 | tf_op jit(solution)/shard_map/ppermute | solution.py:343
  123.7 2.2 %place_shares.2 = (f32[1024,1024]{1,0:T(8,128)}, f32[1024,1024]{1,0:T(8,128)}) custom-call(s32[1]{0:T(128)} %bitcast.1.refs_0_, f32[1024,1024]{1,0:T(8,128)S(1)} %get-tuple-element.24.refs_1_, bf16[128,1024]{1,0:T(8,128)(2,1)S(1)} %level_two.1.refs_2_), custom_call_target="tpu_custom_call" | custom-call | flops 131072 | bytes 786432 | tf_op jit(solution)/shard_map/place_shares/pallas_call | solution.py:322
  125.9 0.1 collective-permute-start
  126.0 2.9 %collective-permute-done.1.refs_2_ = bf16[128,1024]{1,0:T(8,128)(2,1)S(1)} collective-permute-done((bf16[128,1024]{1,0:T(8,128)(2,1)S(1)}, bf16[128,1024]{1,0:T(8,128)(2,1)S(1)}, u32[]{:S(2)}, u32[]{:S(2)}) %collective-permute-start.1) | collective-permute-done | bytes 262176 | tf_op jit(solution)/shard_map/ppermute | solution.py:343
  128.9 4.9 %collective-permute-done.3.refs_4_ = bf16[128,1024]{1,0:T(8,128)(2,1)S(1)} collective-permute-done((bf16[128,1024]{1,0:T(8,128)(2,1)S(1)}, bf16[128,1024]{1,0:T(8,128)(2,1)S(1)}, u32[]{:S(2)}, u32[]{:S(2)}) %collective-permute-start.3) | collective-permute-done | bytes 262176 | tf_op jit(solution)/shard_map/ppermute | solution.py:343
  133.8 0.0 collective-permute-done.5.refs_6_
  133.8 0.0 collective-permute-start.6
  133.8 0.5 collective-permute-start.4
  134.3 0.0 collective-permute-start.2
  134.3 0.0 collective-permute-done.refs_1_
  134.3 1.0 collective-permute-done.6.refs_7_
  135.4 0.4 collective-permute-done.4.refs_5_
  135.7 0.4 collective-permute-done.2.refs_3_
  136.1 1.9 %place_shares.3 = f32[1024,1024]{1,0:T(8,128)} custom-call(s32[1]{0:T(128)} %bitcast.1.refs_0_, bf16[128,1024]{1,0:T(8,128)(2,1)S(1)} %collective-permute-done.refs_1_, bf16[128,1024]{1,0:T(8,128)(2,1)S(1)} %collective-permute-done.1.refs_2_, bf16[128,1024]{1,0:T(8,128)(2,1)S(1)} %collective-permute-done.2.refs_3_, ...), custom_call_target="tpu_custom_call", output_to_operand_aliasing={{}: (8, {})} | custom-call | flops 917504 | bytes 5505024 | tf_op jit(solution)/shard_map/place_shares/pallas_call | solution.py:322
Async XLA Ops:
  0.6 44.9 %copy-start = (f32[1024,1024]{1,0:T(8,128)S(1)}, f32[1024,1024]{1,0:T(8,128)}, u32[]{:S(2)}) copy-start(f32[1024,1024]{1,0:T(8,128)} %refs_2_.3) | copy-start | bytes 12582916
  118.1 10.8 %collective-permute-start.1 = (bf16[128,1024]{1,0:T(8,128)(2,1)S(1)}, bf16[128,1024]{1,0:T(8,128)(2,1)S(1)}, u32[]{:S(2)}, u32[]{:S(2)}) collective-permute-start(bf16[128,1024]{1,0:T(8,128)(2,1)S(1)} %level_two.1.refs_2_), channel_id=1, source_target_pairs={{0,64},{16,80},{32,96},{48,112},{64,0},{80,16},{96,32},{112,48},{1... | collective-permute-start | bytes 786440 | tf_op jit(solution)/shard_map/ppermute | solution.py:343
  120.5 13.3 %collective-permute-start.3 = (bf16[128,1024]{1,0:T(8,128)(2,1)S(1)}, bf16[128,1024]{1,0:T(8,128)(2,1)S(1)}, u32[]{:S(2)}, u32[]{:S(2)}) collective-permute-start(bf16[128,1024]{1,0:T(8,128)(2,1)S(1)} %level_two.1.refs_2_), channel_id=1, source_target_pairs={{0,32},{16,48},{32,64},{48,80},{64,96},{80,112},{96,0},{112,16},{1... | collective-permute-start | bytes 786440 | tf_op jit(solution)/shard_map/ppermute | solution.py:343
  121.3 12.5 %collective-permute-start.5 = (bf16[128,1024]{1,0:T(8,128)(2,1)S(1)}, bf16[128,1024]{1,0:T(8,128)(2,1)S(1)}, u32[]{:S(2)}, u32[]{:S(2)}) collective-permute-start(bf16[128,1024]{1,0:T(8,128)(2,1)S(1)} %level_two.1.refs_2_), channel_id=1, source_target_pairs={{0,96},{16,112},{32,0},{48,16},{64,32},{80,48},{96,64},{112,80},{1... | collective-permute-start | bytes 786440 | tf_op jit(solution)/shard_map/ppermute | solution.py:343
  125.9 8.4 %collective-permute-start = (bf16[128,1024]{1,0:T(8,128)(2,1)S(1)}, bf16[128,1024]{1,0:T(8,128)(2,1)S(1)}, u32[]{:S(2)}, u32[]{:S(2)}) collective-permute-start(bf16[128,1024]{1,0:T(8,128)(2,1)S(1)} %level_two.1.refs_2_), channel_id=1, source_target_pairs={{0,16},{16,0},{32,48},{48,32},{64,80},{80,64},{96,112},{112,96},{1... | collective-permute-start | bytes 786440 | tf_op jit(solution)/shard_map/ppermute | solution.py:341
  133.8 1.5 %collective-permute-start.6 = (bf16[128,1024]{1,0:T(8,128)(2,1)S(1)}, bf16[128,1024]{1,0:T(8,128)(2,1)S(1)}, u32[]{:S(2)}, u32[]{:S(2)}) collective-permute-start(bf16[128,1024]{1,0:T(8,128)(2,1)S(1)} %collective-permute-done.5.refs_6_), channel_id=1, source_target_pairs={{0,16},{16,0},{32,48},{48,32},{64,80},{80,64},{96,112},{112,96},{1... | collective-permute-start | bytes 786440 | tf_op jit(solution)/shard_map/ppermute | solution.py:341
  133.8 1.9 %collective-permute-start.4 = (bf16[128,1024]{1,0:T(8,128)(2,1)S(1)}, bf16[128,1024]{1,0:T(8,128)(2,1)S(1)}, u32[]{:S(2)}, u32[]{:S(2)}) collective-permute-start(bf16[128,1024]{1,0:T(8,128)(2,1)S(1)} %collective-permute-done.3.refs_4_), channel_id=1, source_target_pairs={{0,16},{16,0},{32,48},{48,32},{64,80},{80,64},{96,112},{112,96},{1... | collective-permute-start | bytes 786440 | tf_op jit(solution)/shard_map/ppermute | solution.py:341
  134.3 1.8 %collective-permute-start.2 = (bf16[128,1024]{1,0:T(8,128)(2,1)S(1)}, bf16[128,1024]{1,0:T(8,128)(2,1)S(1)}, u32[]{:S(2)}, u32[]{:S(2)}) collective-permute-start(bf16[128,1024]{1,0:T(8,128)(2,1)S(1)} %collective-permute-done.1.refs_2_), channel_id=1, source_target_pairs={{0,16},{16,0},{32,48},{48,32},{64,80},{80,64},{96,112},{112,96},{1... | collective-permute-start | bytes 786440 | tf_op jit(solution)/shard_map/ppermute | solution.py:341

commit v4 on v3

--- a/solution.py
+++ b/solution.py
@@ -7,6 +7,7 @@
 
 ITER2 = 2
 CAP = 4
+ROWS = 2
 CAP_SHARE = 16
 EXTRA = 128
 DIGIT = 32
@@ -74,10 +75,10 @@
     for copy in copies:
         copy.start()
     iters, n = assign_ref.shape
-    slots = devices * CAP
+    slots = devices * ROWS
     width = points_ref.shape[1]
 
-    spread = onehot(iota((slots, devices), 0) == iota((slots, devices), 1) * CAP)
+    spread = onehot(iota((slots, devices), 0) == iota((slots, devices), 1) * ROWS)
     copies[0].wait()
     parent = parent_ref[...]
     k = parent.shape[1]
@@ -98,15 +99,17 @@
         dest = target // owned
         local = target % owned
         rank = rank_in_bucket(iota((devices, n), 0) == dest)
-        hot = onehot(slot_iota == dest * CAP + rank)
-        lane = iota((EXTRA, n), 0) - 2 * t
-        digits = jnp.where(lane == 0, local // DIGIT + 1, jnp.where(lane == 1, local % DIGIT, 0))
-        extra = extra + nt(hot, digits.astype(F32).astype(BF16))
         if t == 0:
             copies[2].wait()
-        rows = nn(hot, points_ref[...]).reshape(devices, CAP, width)
-        out_ref[:, :, t * width : (t + 1) * width] = rows.astype(BF16)
-    out_ref[:, :, iters * width :] = extra.reshape(devices, CAP, EXTRA).astype(BF16)
+        for h in range(CAP // ROWS):
+            block = t * (CAP // ROWS) + h
+            hot = onehot(slot_iota == jnp.where(rank // ROWS == h, dest * ROWS + rank % ROWS, -1))
+            lane = iota((EXTRA, n), 0) - 2 * block
+            digits = jnp.where(lane == 0, local // DIGIT + 1, jnp.where(lane == 1, local % DIGIT, 0))
+            extra = extra + nt(hot, digits.astype(F32).astype(BF16))
+            rows = nn(hot, points_ref[...]).reshape(devices, ROWS, width)
+            out_ref[:, :, block * width : (block + 1) * width] = rows.astype(BF16)
+    out_ref[:, :, iters * (CAP // ROWS) * width :] = extra.reshape(devices, ROWS, EXTRA).astype(BF16)
 
 
 def lloyd_one_kernel(
@@ -124,13 +127,16 @@
         rounded = old_ref[...].astype(BF16)
         mass = jnp.zeros((1, owned), F32)
         for c in range(0, half, step):
+            part = got_ref.shape[0] * ROWS
+            block, first = t * (CAP // ROWS) + c // part, c % part
+
             def rows(lo, size):
-                got = got_ref[c // CAP : (c + step) // CAP, :, lo : lo + size]
+                got = got_ref[first // ROWS : (first + step) // ROWS, :, lo : lo + size]
                 return got.astype(F32).reshape(step, size)
 
-            extra = rows(iters * width, EXTRA)
-            values = rows(t * width, width)
-            label = ((extra[:, 2 * t : 2 * t + 1] - 1.0) * DIGIT + extra[:, 2 * t + 1 : 2 * t + 2]).astype(jnp.int32)
+            extra = rows(iters * (CAP // ROWS) * width, EXTRA)
+            values = rows(block * width, width)
+            label = ((extra[:, 2 * block : 2 * block + 1] - 1.0) * DIGIT + extra[:, 2 * block + 1 : 2 * block + 2]).astype(jnp.int32)
             mask = iota((step, owned), 1) == label
             member = onehot(mask)
             member_ref[c : c + step, :] = member
@@ -163,8 +169,8 @@
 def member_two(got_ref, member_ref):
     total, share = member_ref.shape
     devices = got_ref.shape[0]
-    slots = devices * CAP
-    first = onehot(iota((devices, slots), 1) == iota((devices, slots), 0) * CAP)
+    slots = devices * ROWS
+    first = onehot(iota((devices, slots), 1) == iota((devices, slots), 0) * ROWS)
     extra = got_ref[:, :, got_ref.shape[2] - EXTRA :].astype(F32).reshape(slots, EXTRA)
     labels = nn(first, extra.astype(BF16)).astype(BF16)
     expand = onehot(iota((total, devices), 0) // CAP_SHARE == iota((total, devices), 1))
@@ -252,7 +258,7 @@
     return pl.pallas_call(
         lambda *refs: pack_one_kernel(devices, owned, share, subs, *refs),
         out_shape=(
-            jax.ShapeDtypeStruct((devices, CAP, iters * points.shape[1] + EXTRA), BF16),
+            jax.ShapeDtypeStruct((devices, ROWS, iters * (CAP // ROWS) * points.shape[1] + EXTRA), BF16),
             jax.ShapeDtypeStruct(parent.shape, jnp.int32),
         ),
         in_specs=[in_hbm()] * 3,

time: 139 us -> 141 us (1.014)
  Pallas kernels: 23.9 us -> 26.2 us
where the time goes in v4:
time: 141 us; the launch traced here: 140 us
  blocking collectives  97 us (69%)
  Pallas kernels  26.2 us (19%)
  waiting for transfers between devices  9.58 us (7%)
  starting transfers between devices  6.18 us (4%)
    all_to_all x1, blocking collectives, shards(): lax.all_to_all(send_two.reshape(devices, CAP_SHARE, width), ('grp', 'sub'...  55.7 us
    all_to_all x1, blocking collectives, shards(): lax.all_to_all(send, ('grp', 'sub'), split_axis=0, concat_axis=0, tiled=T...  41.3 us
    pallas_call x1, Pallas kernels, level_one(): pl.pallas_call(lambda *refs: lloyd_one_kernel(iters, *refs), out_shape=(p...  12.4 us
    ppermute x3, waiting for transfers between devices, gather_shares(): lax.ppermute(own, 'grp', [(g, (g + 2 * k) % groups) for g in range(groups)])  7.82 us
    ppermute x3, starting transfers between devices, gather_shares(): lax.ppermute(own, 'grp', [(g, (g + 2 * k) % groups) for g in range(groups)])  5.57 us
    pallas_call x1, Pallas kernels, level_two(): pl.pallas_call(lloyd_two_kernel, out_shape=jax.ShapeDtypeStruct((share, w...  5.55 us
    pallas_call x1, Pallas kernels, pack_points(): pl.pallas_call(lambda *refs: pack_one_kernel(devices, owned, share, subs,...  4.14 us
    pallas_call x2, Pallas kernels, place(): pl.pallas_call(lambda *refs: kernel(places, groups, *refs), out_shape=out...  4.11 us
  transfers between devices with their start and end apart: 7, of which 5 were waited for; matrix products, arithmetic and copies ran while one was open for 0% of the time, Pallas kernels for 2%

profile of v4, /device:TPU:0, one launch (start us, length us, event | category | flops | bytes accessed | tf_op | source)
XLA Modules:
  0.0 139.8 jit_solution(6414372996686351753)
XLA Ops:
  0.6 0.0 copy-start
  0.6 4.1 %pack_points.1 = (bf16[128,2,4224]{2,1,0:T(2,128)(2,1)S(1)}, s32[1,1024]{1,0:T(1,128)S(1)}) custom-call(s32[2,256]{1,0:T(2,128)} %refs_0_.1, s32[1,1024]{1,0:T(1,128)} %bitcast.6, bf16[256,1024]{1,0:T(8,128)(2,1)} %refs_2_.2), custom_call_target="tpu_custom_call" | custom-call | tf_op jit(solution)/shard_map/pack_points/pallas_call | solution.py:258
  4.8 41.3 %all_to_all.10.refs_1_ = bf16[128,2,4224]{2,1,0:T(2,128)(2,1)S(1)} all-to-all(bf16[128,2,4224]{2,1,0:T(2,128)(2,1)S(1)} %get-tuple-element.22), channel_id=1, replica_groups=mesh['grp'=8,'sub'=16] {'grp','sub'}, dimensions={0} | all-to-all | bytes 4325376 | tf_op jit(solution)/shard_map/all_to_all | solution.py:372
  46.1 0.0 copy-done
  46.1 12.4 %level_one.1 = (f32[1024,1024]{1,0:T(8,128)S(1)}, bf16[2048,1024]{1,0:T(8,128)(2,1)S(1)}, bf16[2048,128]{1,0:T(8,128)(2,1)S(1)}, f32[128,1024]{1,0:T(8,128)S(1)}) custom-call(s32[1]{0:T(128)} %bitcast.1.refs_0_, bf16[128,2,4224]{2,1,0:T(2,128)(2,1)S(1)} %all_to_all.10.refs_1_, f32[1024,1024]{1,0:T(8,128)S(1)} %copy-done, ...), custom_call_target="tpu_custom_call" | custom-call | tf_op jit(solution)/shard_map/level_one/pallas_call | solution.py:281
  58.6 55.7 %all_to_all.11 = bf16[128,16,1024]{2,1,0:T(8,128)(2,1)S(1)} all-to-all(bf16[128,16,1024]{2,1,0:T(8,128)(2,1)S(1)} %bitcast.5), channel_id=1, replica_groups=mesh['grp'=8,'sub'=16] {'grp','sub'}, dimensions={0} | all-to-all | bytes 8388608 | tf_op jit(solution)/shard_map/all_to_all | solution.py:376
  114.2 5.5 %level_two.1.refs_2_ = bf16[128,1024]{1,0:T(8,128)(2,1)S(1)} custom-call(bf16[2048,1024]{1,0:T(8,128)(2,1)S(1)} %bitcast.4, bf16[2048,128]{1,0:T(8,128)(2,1)S(1)} %get-tuple-element.26.member_ref, f32[128,1024]{1,0:T(8,128)S(1)} %get-tuple-element.27.centers_ref), custom_call_target="tpu_custom_call" | custom-call | tf_op jit(solution)/shard_map/level_two/pallas_call | solution.py:304
  119.8 2.3 %collective-permute-start.1 = (bf16[128,1024]{1,0:T(8,128)(2,1)S(1)}, bf16[128,1024]{1,0:T(8,128)(2,1)S(1)}, u32[]{:S(2)}, u32[]{:S(2)}) collective-permute-start(bf16[128,1024]{1,0:T(8,128)(2,1)S(1)} %level_two.1.refs_2_), channel_id=1, source_target_pairs={{0,64},{16,80},{32,96},{48,112},{64,0},{80,16},{96,32},{112,48},{1... | collective-permute-start | bytes 786440 | tf_op jit(solution)/shard_map/ppermute | solution.py:349
  122.1 0.8 collective-permute-start.3
  122.9 2.4 %collective-permute-start.5 = (bf16[128,1024]{1,0:T(8,128)(2,1)S(1)}, bf16[128,1024]{1,0:T(8,128)(2,1)S(1)}, u32[]{:S(2)}, u32[]{:S(2)}) collective-permute-start(bf16[128,1024]{1,0:T(8,128)(2,1)S(1)} %level_two.1.refs_2_), channel_id=1, source_target_pairs={{0,96},{16,112},{32,0},{48,16},{64,32},{80,48},{96,64},{112,80},{1... | collective-permute-start | bytes 786440 | tf_op jit(solution)/shard_map/ppermute | solution.py:349
  125.3 2.2 %place_shares.2 = (f32[1024,1024]{1,0:T(8,128)}, f32[1024,1024]{1,0:T(8,128)}) custom-call(s32[1]{0:T(128)} %bitcast.1.refs_0_, f32[1024,1024]{1,0:T(8,128)S(1)} %get-tuple-element.24.refs_1_, bf16[128,1024]{1,0:T(8,128)(2,1)S(1)} %level_two.1.refs_2_), custom_call_target="tpu_custom_call" | custom-call | flops 131072 | bytes 786432 | tf_op jit(solution)/shard_map/place_shares/pallas_call | solution.py:328
  127.5 0.1 collective-permute-start
  127.6 2.9 %collective-permute-done.1.refs_2_ = bf16[128,1024]{1,0:T(8,128)(2,1)S(1)} collective-permute-done((bf16[128,1024]{1,0:T(8,128)(2,1)S(1)}, bf16[128,1024]{1,0:T(8,128)(2,1)S(1)}, u32[]{:S(2)}, u32[]{:S(2)}) %collective-permute-start.1) | collective-permute-done | bytes 262176 | tf_op jit(solution)/shard_map/ppermute | solution.py:349
  130.5 4.9 %collective-permute-done.3.refs_4_ = bf16[128,1024]{1,0:T(8,128)(2,1)S(1)} collective-permute-done((bf16[128,1024]{1,0:T(8,128)(2,1)S(1)}, bf16[128,1024]{1,0:T(8,128)(2,1)S(1)}, u32[]{:S(2)}, u32[]{:S(2)}) %collective-permute-start.3) | collective-permute-done | bytes 262176 | tf_op jit(solution)/shard_map/ppermute | solution.py:349
  135.5 0.0 collective-permute-done.5.refs_6_
  135.5 0.0 collective-permute-start.6
  135.5 0.5 collective-permute-start.4
  136.0 0.0 collective-permute-start.2
  136.0 0.0 collective-permute-done.refs_1_
  136.0 1.0 collective-permute-done.6.refs_7_
  137.0 0.4 collective-permute-done.4.refs_5_
  137.4 0.4 collective-permute-done.2.refs_3_
  137.7 1.9 %place_shares.3 = f32[1024,1024]{1,0:T(8,128)} custom-call(s32[1]{0:T(128)} %bitcast.1.refs_0_, bf16[128,1024]{1,0:T(8,128)(2,1)S(1)} %collective-permute-done.refs_1_, bf16[128,1024]{1,0:T(8,128)(2,1)S(1)} %collective-permute-done.1.refs_2_, bf16[128,1024]{1,0:T(8,128)(2,1)S(1)} %collective-permute-done.2.refs_3_, ...), custom_call_target="tpu_custom_call", output_to_operand_aliasing={{}: (8, {})} | custom-call | flops 917504 | bytes 5505024 | tf_op jit(solution)/shard_map/place_shares/pallas_call | solution.py:328
Async XLA Ops:
  0.6 45.5 %copy-start = (f32[1024,1024]{1,0:T(8,128)S(1)}, f32[1024,1024]{1,0:T(8,128)}, u32[]{:S(2)}) copy-start(f32[1024,1024]{1,0:T(8,128)} %refs_2_.3) | copy-start | bytes 12582916
  119.8 10.8 %collective-permute-start.1 = (bf16[128,1024]{1,0:T(8,128)(2,1)S(1)}, bf16[128,1024]{1,0:T(8,128)(2,1)S(1)}, u32[]{:S(2)}, u32[]{:S(2)}) collective-permute-start(bf16[128,1024]{1,0:T(8,128)(2,1)S(1)} %level_two.1.refs_2_), channel_id=1, source_target_pairs={{0,64},{16,80},{32,96},{48,112},{64,0},{80,16},{96,32},{112,48},{1... | collective-permute-start | bytes 786440 | tf_op jit(solution)/shard_map/ppermute | solution.py:349
  122.1 13.3 %collective-permute-start.3 = (bf16[128,1024]{1,0:T(8,128)(2,1)S(1)}, bf16[128,1024]{1,0:T(8,128)(2,1)S(1)}, u32[]{:S(2)}, u32[]{:S(2)}) collective-permute-start(bf16[128,1024]{1,0:T(8,128)(2,1)S(1)} %level_two.1.refs_2_), channel_id=1, source_target_pairs={{0,32},{16,48},{32,64},{48,80},{64,96},{80,112},{96,0},{112,16},{1... | collective-permute-start | bytes 786440 | tf_op jit(solution)/shard_map/ppermute | solution.py:349
  122.9 12.5 %collective-permute-start.5 = (bf16[128,1024]{1,0:T(8,128)(2,1)S(1)}, bf16[128,1024]{1,0:T(8,128)(2,1)S(1)}, u32[]{:S(2)}, u32[]{:S(2)}) collective-permute-start(bf16[128,1024]{1,0:T(8,128)(2,1)S(1)} %level_two.1.refs_2_), channel_id=1, source_target_pairs={{0,96},{16,112},{32,0},{48,16},{64,32},{80,48},{96,64},{112,80},{1... | collective-permute-start | bytes 786440 | tf_op jit(solution)/shard_map/ppermute | solution.py:349
  127.5 8.4 %collective-permute-start = (bf16[128,1024]{1,0:T(8,128)(2,1)S(1)}, bf16[128,1024]{1,0:T(8,128)(2,1)S(1)}, u32[]{:S(2)}, u32[]{:S(2)}) collective-permute-start(bf16[128,1024]{1,0:T(8,128)(2,1)S(1)} %level_two.1.refs_2_), channel_id=1, source_target_pairs={{0,16},{16,0},{32,48},{48,32},{64,80},{80,64},{96,112},{112,96},{1... | collective-permute-start | bytes 786440 | tf_op jit(solution)/shard_map/ppermute | solution.py:347
  135.5 1.5 %collective-permute-start.6 = (bf16[128,1024]{1,0:T(8,128)(2,1)S(1)}, bf16[128,1024]{1,0:T(8,128)(2,1)S(1)}, u32[]{:S(2)}, u32[]{:S(2)}) collective-permute-start(bf16[128,1024]{1,0:T(8,128)(2,1)S(1)} %collective-permute-done.5.refs_6_), channel_id=1, source_target_pairs={{0,16},{16,0},{32,48},{48,32},{64,80},{80,64},{96,112},{112,96},{1... | collective-permute-start | bytes 786440 | tf_op jit(solution)/shard_map/ppermute | solution.py:347
  135.5 1.9 %collective-permute-start.4 = (bf16[128,1024]{1,0:T(8,128)(2,1)S(1)}, bf16[128,1024]{1,0:T(8,128)(2,1)S(1)}, u32[]{:S(2)}, u32[]{:S(2)}) collective-permute-start(bf16[128,1024]{1,0:T(8,128)(2,1)S(1)} %collective-permute-done.3.refs_4_), channel_id=1, source_target_pairs={{0,16},{16,0},{32,48},{48,32},{64,80},{80,64},{96,112},{112,96},{1... | collective-permute-start | bytes 786440 | tf_op jit(solution)/shard_map/ppermute | solution.py:347
  136.0 1.8 %collective-permute-start.2 = (bf16[128,1024]{1,0:T(8,128)(2,1)S(1)}, bf16[128,1024]{1,0:T(8,128)(2,1)S(1)}, u32[]{:S(2)}, u32[]{:S(2)}) collective-permute-start(bf16[128,1024]{1,0:T(8,128)(2,1)S(1)} %collective-permute-done.1.refs_2_), channel_id=1, source_target_pairs={{0,16},{16,0},{32,48},{48,32},{64,80},{80,64},{96,112},{112,96},{1... | collective-permute-start | bytes 786440 | tf_op jit(solution)/shard_map/ppermute | solution.py:347
